TPU v7x, 256 devices: a whole 4x4x8 slice. The times are simulated.
256 devices in a mesh: cells: 64 (over z, x, core), genes: 4 (over y).
Axes of the slice: x: 4, y: 4, z: 8, core: 2. Of those that a mesh axis runs over, the one named last changes fastest.
Arguments:
- expression: bfloat16 [65536, 2048], P('cells', 'genes'), may hold values from -6 to 6
- affinity: bfloat16 [512, 12, 128, 128], P('cells'), may hold values from -0.15625 to 0.15625
- near_blocks: int32 [512, 4], P('cells'), may hold values from 0 to 511, as said below
- far_blocks: int32 [512, 8], P('cells'), may hold values from 0 to 511, as said below
- far_count: int32 [512], P('cells'), may hold values from 1 to 8, as said below
Outputs:
- smoothed: bfloat16 [65536, 2048], P('cells', 'genes')
- covariance: float32 [2048, 2048], P('cells', 'genes')
Inputs may be any that keep to these rules, and one draw needn't show every extreme that they name: near_blocks[b, 0] = b, and every entry names a block of the same shard of 8 consecutive blocks as b. `far_blocks`: over the 8 x 8 entries of the blocks of one shard, every shard owns exactly 1 of the named blocks; a block may be named more than once. `far_count`: in every draw some shard has all its counts equal to 8.
All inputs are finite; a program needn't handle non-finite values.
Results may differ from a plain program's by a relative error of at most 0.0049.
Values may be sent and summed in bfloat16 or wider, within the bound.
A program may use at most 192 MiB of HBM per device.

v0:
```python
import jax
import jax.numpy as jnp
from jax import lax
from jax.sharding import PartitionSpec as P

STEPS = 2


def peer_ranks(owners):
    positions = jnp.arange(owners.shape[0], dtype=jnp.int32)
    same_owner = owners[:, None] == owners[None, :]
    earlier = positions[None, :] < positions[:, None]
    return jnp.sum((same_owner & earlier).astype(jnp.int32), axis=1)


def body(expression, affinity, near_blocks, far_blocks, far_count):
    shard_total = lax.axis_size("cells")
    cell_rows, gene_cols = expression.shape
    block_size = affinity.shape[2]
    local_blocks = cell_rows // block_size
    near_slots = near_blocks.shape[1]
    far_slots = far_blocks.shape[1]
    capacity = local_blocks * far_slots // shard_total
    owners = (far_blocks // local_blocks).reshape(-1)
    local_index = (far_blocks % local_blocks).reshape(-1)
    ranks = peer_ranks(owners)
    live_slots = jnp.arange(far_slots, dtype=jnp.int32)[None, :] < far_count[:, None]
    slot_mask = jnp.concatenate(
        [jnp.ones((local_blocks, near_slots), dtype=bool), live_slots], axis=1
    )
    weights = jnp.where(slot_mask[:, :, None, None], affinity, jnp.zeros_like(affinity))
    near_weights = weights[:, :near_slots]
    far_weights = weights[:, near_slots:]
    near_local = near_blocks % local_blocks
    table = jnp.zeros((shard_total, capacity), jnp.int32).at[owners, ranks].set(local_index)
    asked = lax.all_to_all(table, "cells", split_axis=0, concat_axis=0, tiled=True)
    current = expression
    for iteration in range(STEPS):
        blocks = current.reshape(local_blocks, block_size, gene_cols)
        near_part = blocks[near_local]
        accumulated = jnp.einsum(
            "bkij,bkjg->big", near_weights, near_part, preferred_element_type=jnp.float32
        )
        replies = blocks[asked]
        received = lax.all_to_all(replies, "cells", split_axis=0, concat_axis=0, tiled=True)
        far_part = received[owners, ranks].reshape(local_blocks, far_slots, block_size, gene_cols)
        accumulated = accumulated + jnp.einsum(
            "bkij,bkjg->big", far_weights, far_part, preferred_element_type=jnp.float32
        )
        current = accumulated.reshape(cell_rows, gene_cols).astype(jnp.bfloat16)
    whole = lax.all_gather(current, "genes", axis=1, tiled=True)
    summed = lax.psum_scatter(
        lax.dot_general(
            whole, current, (((0,), (0,)), ((), ())), preferred_element_type=jnp.float32
        ),
        "cells",
        scatter_dimension=0,
        tiled=True,
    )
    covariance = summed / (cell_rows * shard_total)
    return (current, covariance)


def solution(mesh):
    return jax.shard_map(
        body,
        mesh=mesh,
        in_specs=(
            P("cells", "genes"),
            P("cells", None, None, None),
            P("cells", None),
            P("cells", None),
            P("cells"),
        ),
        out_specs=(P("cells", "genes"), P("cells", "genes")),
        check_vma=False,
    )
```

profile of v0, /device:TPU:33, one launch (start us, length us, event | category | flops | bytes accessed | tf_op | source)
XLA Modules:
  0.0 659.9 jit_solution(338175133138309200)
XLA Ops:
  7.2 0.8 add_select_fusion
  8.4 0.8 scatter_custom_fusion
  9.3 20.0 %all_to_all.19 = s32[64,1,1]{2,1,0:T(1,128)S(1)} all-to-all(s32[64,1,1]{2,1,0:T(1,128)S(1)} %copy.16), channel_id=1, replica_groups=mesh['cells'=64,'genes'=4] {'cells'}, dimensions={0} | all-to-all | bytes 512 | tf_op jit(solution)/shard_map/all_to_all | solution.py:36
  29.3 1.2 fusion.10
  30.6 5.5 gather_fusion.1
  36.1 6.7 %all-to-all-start.1 = ((bf16[64,1,128,512]{3,2,1,0:T(8,128)(2,1)}), bf16[64,1,128,512]{3,2,1,0:T(8,128)(2,1)}, u32[]{:S(2)}, u32[]{:S(2)}) async-start(bf16[64,1,128,512]{3,2,1,0:T(8,128)(2,1)} %bitcast.45), calls=%async_computation.1 | async-start | bytes 16777216 | tf_op jit(solution)/shard_map/all_to_all | solution.py:45
  43.0 2.8 gather_fusion
  46.0 182.8 %all-to-all-done.1 = bf16[64,1,128,512]{3,2,1,0:T(8,128)(2,1)} async-done(((bf16[64,1,128,512]{3,2,1,0:T(8,128)(2,1)}), bf16[64,1,128,512]{3,2,1,0:T(8,128)(2,1)}, u32[]{:S(2)}, u32[]{:S(2)}) %all-to-all-start.1) | async-done | bytes 8388640 | tf_op jit(solution)/shard_map/all_to_all | solution.py:45
  228.8 9.1 %gather_fusion.2 = bf16[64,128,512]{2,1,0:T(8,128)(2,1)} fusion(bf16[64,1,128,512]{3,2,1,0:T(8,128)(2,1)} %all-to-all-done.1, s32[64]{0:T(128)S(1)} %get-tuple-element.4), kind=kCustom, calls=%fused_computation.2 | custom fusion | bytes 16777728 | tf_op jit(solution)/shard_map/gather | solution.py:46
  237.9 4.8 fusion.2
  242.7 0.7 copy-done.5
  243.4 0.8 fusion.1
  244.2 5.5 gather_fusion.4
  249.7 6.8 %all-to-all-start.2 = ((bf16[64,1,128,512]{3,2,1,0:T(8,128)(2,1)}), bf16[64,1,128,512]{3,2,1,0:T(8,128)(2,1)}, u32[]{:S(2)}, u32[]{:S(2)}) async-start(bf16[64,1,128,512]{3,2,1,0:T(8,128)(2,1)} %bitcast.46), calls=%async_computation.2 | async-start | bytes 16777216 | tf_op jit(solution)/shard_map/all_to_all | solution.py:45
  256.5 0.2 all-gather.2.cloned.1.call-start
  256.8 2.8 gather_fusion.3
  259.5 182.9 %all-to-all-done.2 = bf16[64,1,128,512]{3,2,1,0:T(8,128)(2,1)} async-done(((bf16[64,1,128,512]{3,2,1,0:T(8,128)(2,1)}), bf16[64,1,128,512]{3,2,1,0:T(8,128)(2,1)}, u32[]{:S(2)}, u32[]{:S(2)}) %all-to-all-start.2) | async-done | bytes 8388640 | tf_op jit(solution)/shard_map/all_to_all | solution.py:45
  442.4 9.0 %gather_fusion.5 = bf16[64,128,512]{2,1,0:T(8,128)(2,1)} fusion(bf16[64,1,128,512]{3,2,1,0:T(8,128)(2,1)} %all-to-all-done.2, s32[64]{0:T(128)S(1)} %get-tuple-element.4), kind=kCustom, calls=%fused_computation.5 | custom fusion | bytes 16777728 | tf_op jit(solution)/shard_map/gather | solution.py:46
  451.4 4.8 fusion.4
  456.2 1.8 fusion
  458.1 48.2 %all-gather.2.cloned.1.call-done = bf16[1024,2048]{1,0:T(8,128)(2,1)} async-done(((bf16[1024,512]{1,0:T(8,128)(2,1)}), bf16[1024,2048]{1,0:T(8,128)(2,1)}) %all-gather.2.cloned.1.call-update) | async-done | bytes 4194320 | tf_op jit(solution)/shard_map/all_gather | solution.py:51
  506.3 6.9 %fusion.22 = f32[2048,512]{1,0:T(8,128)} fusion(bf16[1024,2048]{1,0:T(8,128)(2,1)} %all-gather.2.cloned.1.call-done, bf16[1024,512]{1,0:T(8,128)(2,1)} %bitcast.52), kind=kOutput, calls=%fused_computation.53 | convolution fusion | flops 2147483648 | bytes 9437184 | tf_op jit(solution)/shard_map/dot_general | solution.py:53
  513.2 138.4 %reduce-scatter.2.cloned.1.call-done = f32[32,512]{1,0:T(8,128)} async-done(((f32[2048,512]{1,0:T(8,128)}), f32[32,512]{1,0:T(8,128)}) %reduce-scatter.2.cloned.1.call-update) | async-done | bytes 65552 | tf_op jit(solution)/shard_map/reduce_scatter | solution.py:52
  651.6 1.5 broadcast_multiply_fusion
  (33 shorter events, 1.0 us)
Async XLA Ops:
  7.2 23.4 %copy-start = (bf16[1024,512]{1,0:T(8,128)(2,1)S(1)}, bf16[1024,512]{1,0:T(8,128)(2,1)}, u32[]{:S(2)}) copy-start(bf16[1024,512]{1,0:T(8,128)(2,1)} %param.5) | copy-start | bytes 3145732
  36.1 6.7 %copy-start.7 = (s32[8,4]{0,1:T(4,128)S(1)}, s32[8,4]{0,1:T(4,128)}, u32[]{:S(2)}) copy-start(s32[8,4]{0,1:T(4,128)} %param.7) | copy-start | bytes 388
  36.1 192.7 %all-to-all-start.1 = ((bf16[64,1,128,512]{3,2,1,0:T(8,128)(2,1)}), bf16[64,1,128,512]{3,2,1,0:T(8,128)(2,1)}, u32[]{:S(2)}, u32[]{:S(2)}) async-start(bf16[64,1,128,512]{3,2,1,0:T(8,128)(2,1)} %bitcast.45), calls=%async_computation.1 | async-start | bytes 16777216 | tf_op jit(solution)/shard_map/all_to_all | solution.py:45
  43.0 2.8 copy-start.8
  228.7 9.1 %copy-start.2 = (bf16[8,12,128,128]{3,2,1,0:T(8,128)(2,1)S(1)}, bf16[8,12,128,128]{3,2,1,0:T(8,128)(2,1)}, u32[]{:S(2)}) copy-start(bf16[8,12,128,128]{3,2,1,0:T(8,128)(2,1)} %param.6) | copy-start | bytes 9437188
  237.9 4.8 copy-start.3
  237.9 5.5 copy-start.5
  249.7 192.7 %all-to-all-start.2 = ((bf16[64,1,128,512]{3,2,1,0:T(8,128)(2,1)}), bf16[64,1,128,512]{3,2,1,0:T(8,128)(2,1)}, u32[]{:S(2)}, u32[]{:S(2)}) async-start(bf16[64,1,128,512]{3,2,1,0:T(8,128)(2,1)} %bitcast.46), calls=%async_computation.2 | async-start | bytes 16777216 | tf_op jit(solution)/shard_map/all_to_all | solution.py:45
  256.5 249.8 %all-gather.2.cloned.1.call-start = ((), (), s32[]{:S(2)}) async-start(), calls=%async_computation.4 | async-start | bytes 5242880 | tf_op jit(solution)/shard_map/all_gather | solution.py:51
  259.5 191.9 %copy-start.4 = (bf16[8,12,128,128]{3,2,1,0:T(8,128)(2,1)S(1)}, bf16[8,12,128,128]{3,2,1,0:T(8,128)(2,1)}, u32[]{:S(2)}) copy-start(bf16[8,12,128,128]{3,2,1,0:T(8,128)(2,1)} %param.6) | copy-start | bytes 9437188
  451.4 4.8 copy-start.6
  458.1 193.5 %reduce-scatter.2.cloned.1.call-start = ((), (), s32[]{:S(2)}) async-start(), calls=%async_computation.5 | async-start | bytes 4259840 | tf_op jit(solution)/shard_map/reduce_scatter | solution.py:52
  506.3 146.8 %copy-start.1 = (bf16[1024,512]{1,0:T(8,128)(2,1)S(1)}, bf16[1024,512]{1,0:T(8,128)(2,1)}, u32[]{:S(2)}) copy-start(bf16[1024,512]{1,0:T(8,128)(2,1)} %param.5) | copy-start | bytes 3145732
Sparse Core Ops, SparseCore 0:
  458.2 48.0 all-gather.1
  513.4 138.1 reduce-scatter.1
where the time goes:
time: 667 us; the launch traced here: 660 us
  waiting for transfers between devices  552 us (83%)
  local copies, waits for them, and re-layouts  36.8 us (6%)
  blocking collectives  20 us (3%)
  matrix products  19.1 us (3%)
  between operations  14.2 us (2%)
  starting transfers between devices  13.8 us (2%)
    all_to_all x2, waiting for transfers between devices, body(): lax.all_to_all(replies, 'cells', split_axis=0, concat_axis=0, tiled=True)  366 us
    reduce_scatter x1, waiting for transfers between devices, body(): lax.psum_scatter(lax.dot_general(whole, current, (((0,), (0,)), ((), ()))...  138 us
    all_gather x1, waiting for transfers between devices, body(): whole = lax.all_gather(current, 'genes', axis=1, tiled=True)  48.2 us
    all_to_all x1, blocking collectives, body(): lax.all_to_all(table, 'cells', split_axis=0, concat_axis=0, tiled=True)  20 us
    gather x2, local copies, waits for them, and re-layouts, body(): received[owners, ranks]  18.1 us
    all_to_all x2, starting transfers between devices, body(): lax.all_to_all(replies, 'cells', split_axis=0, concat_axis=0, tiled=True)  13.5 us
  transfers between devices with their start and end apart: 4, of which 4 were waited for; matrix products, arithmetic and copies ran while one was open for 1% of the time, Pallas kernels for 0%

commit v1 on v0

v1 whole, which is shorter than its diff:
```python
import functools

import jax
import jax.numpy as jnp
from jax import lax
from jax.experimental import pallas as pl
from jax.experimental.pallas import tpu as pltpu
from jax.sharding import PartitionSpec as P

MESH = pl.DeviceIdType.MESH
NX = 4
NY = 4
BL = 128
BLK = 8
SLOTS = 12


def remote(src, dst, send, recv, device):
    return pltpu.make_async_remote_copy(
        src_ref=src, dst_ref=dst, send_sem=send, recv_sem=recv, device_id=device, device_id_type=MESH
    )


def diffuse_kernel(
    nz, expr, aff, lists, out, x0, x1, x2, w, lv, ls,
    loc, xs_s, xs_r, li_s, li_r, wx_s, wx_r, wf_s, wf_r, wy_s, wy_r,
    z_s, z_r, p_s, p_r, o_s, o_r,
):
    flow_len = 4 * (nz // 2) - 2
    me = lax.axis_index("cells")
    y = lax.axis_index("genes")
    core = lax.rem(me, 2)
    x = lax.rem(me // 2, NX)
    z = me // (2 * NX)
    half = lax.rem(y, 2)

    def cell(zz, xx, kk):
        return (zz * NX + xx) * 2 + kk

    def wrap(v, n):
        return lax.rem(v + n, n)

    def x_dev(d):
        return (cell(z, wrap(x + d, NX), core), y)

    right = (cell(wrap(z + 1, nz), x, core), y)
    left = (cell(wrap(z - 1, nz), x, core), y)
    partner = (cell(z, x, 1 - core), y)
    up = (me, wrap(y + 1, NY))
    down = (me, wrap(y - 1, NY))

    barrier = pltpu.get_barrier_semaphore()
    peers = [x_dev(1), x_dev(2), x_dev(3), right, left, partner, up, down]
    for peer in peers:
        pl.semaphore_signal(barrier, inc=1, device_id=peer, device_id_type=MESH)
    pl.semaphore_wait(barrier, len(peers))

    def piece(buf, shard):
        return buf.at[pl.ds(shard * BLK, BLK)]

    def columns(ref, xx):
        return ref.at[:, :, pl.ds(pl.multiple_of(xx * BL, BL), BL)]

    def deal(d):
        return remote(
            columns(expr, wrap(x + d, NX)), piece(x0, me), xs_s.at[d - 1], xs_r.at[d - 1], x_dev(d)
        )

    own_in = pltpu.make_async_copy(columns(expr, x), piece(x0, me), loc.at[0])
    own_in.start()
    for d in (1, 3, 2):
        deal(d).start()

    def names(d):
        return remote(lists, lv.at[x], li_s.at[d - 1], li_r.at[d - 1], x_dev(d))

    own_names = pltpu.make_async_copy(lists, lv.at[x], loc.at[1])
    own_names.start()
    for d in (1, 2, 3):
        names(d).start()

    own_w = pltpu.make_async_copy(aff, w.at[x], loc.at[2])

    def wsub(xx, hh, u):
        return w.at[xx, pl.ds(4 * hh + 2 * u, 2)]

    def w_first(way, u):
        return remote(
            aff.at[pl.ds(4 * half + 2 * u, 2)], wsub(x, half, u),
            wx_s.at[way, u], wx_r.at[way, u], x_dev(1 if way == 0 else 3),
        )

    def w_forward(way):
        ref = wsub(wrap(x - 1, NX), half, 0) if way == 0 else wsub(wrap(x + 1, NX), half, 1)
        return remote(ref, ref, wf_s.at[way], wf_r.at[way], x_dev(1 if way == 0 else 3))

    def w_across(e, u):
        ref = wsub(wrap(x + (3, 1, 2)[e], NX), half, u)
        return remote(ref, ref, wy_s.at[u, e], wy_r.at[u, e], up if u == 0 else down)

    for way, u in ((0, 0), (1, 1), (0, 1), (1, 0)):
        w_first(way, u).start()
    own_w.start()

    def w_serve(stage):
        if stage == 0:
            w_first(0, 0).wait_recv()
            w_forward(0).start()
            w_across(0, 0).start()
            w_first(1, 1).wait_recv()
            w_forward(1).start()
            w_across(1, 1).start()
        elif stage == 1:
            w_first(0, 1).wait_recv()
            w_across(0, 1).start()
            w_first(1, 0).wait_recv()
            w_across(1, 0).start()
        else:
            w_forward(0).wait_recv()
            w_across(2, 0).start()
            w_forward(1).wait_recv()
            w_across(2, 1).start()

    def shard_of(zz, j, kk):
        return cell(wrap(zz, nz), wrap(x - j, NX), kk)

    def z_copy(n, buf, way, s, shard):
        return remote(
            piece(buf, shard), piece(buf, shard), z_s.at[n, way, s], z_r.at[n, way, s],
            right if way == 0 else left,
        )

    def p_copy(n, buf, q, shard):
        return remote(piece(buf, shard), piece(buf, shard), p_s.at[n, q], p_r.at[n, q], partner)

    def from_left(r, kk):
        return shard_of(z - 1 - r // 4, lax.rem(r, 4), kk)

    def from_right(r, kk):
        j = lax.rem(r, 4) + jnp.where(r < flow_len - 2, 0, 2)
        return shard_of(z + 1 + r // 4, j, kk)

    def send_own(n, buf, j):
        shard = shard_of(z, j, core)
        z_copy(n, buf, 0, j, shard).start()
        z_copy(n, buf, 1, j, shard).start()
        p_copy(n, buf, j, shard).start()

    def pass_on(n, buf, first, last):
        @pl.loop(first, last)
        def _(r):
            shard = from_left(r, core)
            z_copy(n, buf, 0, r, shard).wait_recv()

            @pl.when(r + 4 < flow_len)
            def _():
                z_copy(n, buf, 0, r + 4, shard).start()

            p_copy(n, buf, 4 + r, shard).start()
            other = from_right(r, core)
            z_copy(n, buf, 1, r, other).wait_recv()

            @pl.when(r < flow_len - 6)
            def _():
                z_copy(n, buf, 1, r + 4, other).start()

            @pl.when((r >= flow_len - 4) & (r < flow_len - 2))
            def _():
                z_copy(n, buf, 1, r + 2, other).start()

            p_copy(n, buf, 4 + flow_len + r, other).start()

    def partner_done(n, buf):
        @pl.loop(0, 4)
        def _(j):
            p_copy(n, buf, j, shard_of(z, j, 1 - core)).wait_recv()

        @pl.loop(0, flow_len)
        def _(r):
            p_copy(n, buf, 4 + r, from_left(r, 1 - core)).wait_recv()
            p_copy(n, buf, 4 + flow_len + r, from_right(r, 1 - core)).wait_recv()

    def sends_done(n, buf):
        shard = shard_of(z, 0, core)

        @pl.loop(0, flow_len)
        def _(s):
            z_copy(n, buf, 0, s, shard).wait_send()
            z_copy(n, buf, 1, s, shard).wait_send()

        @pl.loop(0, 4 + 2 * flow_len)
        def _(q):
            p_copy(n, buf, q, shard).wait_send()

    def block_sum(buf, xs, b):
        total = None
        for pair in range(SLOTS // 2):
            rows = [buf[ls[xs, b, 2 * pair + i]] for i in range(2)]
            mats = [w[xs, b, 2 * pair + i] for i in range(2)]
            term = jnp.dot(
                jnp.concatenate(mats, axis=1), jnp.concatenate(rows, axis=0),
                preferred_element_type=jnp.float32,
            )
            total = term if total is None else total + term
        return total.astype(jnp.bfloat16)

    zeros = jnp.zeros((BL, BL), jnp.bfloat16)
    x0[nz * 2 * NX * BLK] = zeros
    x1[nz * 2 * NX * BLK] = zeros

    own_in.wait()
    send_own(0, x0, 0)
    for j in (1, 3, 2):
        deal(j).wait_recv()
        send_own(0, x0, j)
    cuts = (0, flow_len // 2 - 1, flow_len // 2 + 2, flow_len - 1, flow_len)
    for part in range(4):
        pass_on(0, x0, cuts[part], cuts[part + 1])
        if part < 3:
            w_serve(part)

    own_names.wait()
    for d in (1, 2, 3):
        names(d).wait_recv()
    to_smem = pltpu.make_async_copy(lv, ls, loc.at[1])
    to_smem.start()
    to_smem.wait()
    own_w.wait()
    partner_done(0, x0)
    for e in range(3):
        for u in range(2):
            w_across(e, u).wait_recv()

    @pl.loop(0, NX)
    def _(j):
        xs = wrap(x - j, NX)
        base = shard_of(z, j, core) * BLK

        @pl.loop(0, BLK)
        def _(b):
            x1[base + b] = block_sum(x0, xs, b)

        send_own(1, x1, j)

    pass_on(1, x1, 0, flow_len)
    partner_done(1, x1)

    def give(j):
        return remote(
            x2.at[j], columns(out, x), o_s.at[j - 1], o_r.at[j - 1],
            (cell(z, wrap(x - j, NX), core), y),
        )

    @pl.loop(0, NX)
    def _(j):
        xs = wrap(x - j, NX)

        @pl.loop(0, BLK)
        def _(b):
            x2[j, b] = block_sum(x1, xs, b)

        @pl.when(j > 0)
        def _():
            give(j).start()

    own_out = pltpu.make_async_copy(x2.at[0], columns(out, x), loc.at[0])
    own_out.start()

    for d in (1, 2, 3):
        deal(d).wait_send()
        names(d).wait_send()
        for u in range(2):
            w_across(d - 1, u).wait_send()
    for way in range(2):
        w_forward(way).wait_send()
        for u in range(2):
            w_first(way, u).wait_send()
    sends_done(0, x0)
    sends_done(1, x1)
    own_out.wait()
    for j in (1, 2, 3):
        give(j).wait()


def diffuse(expression, affinity, lists, nz):
    shards = nz * 2 * NX
    flow_len = 4 * (nz // 2) - 2
    dma = pltpu.SemaphoreType.DMA
    any_spec = pl.BlockSpec(memory_space=pl.ANY)
    return pl.pallas_call(
        functools.partial(diffuse_kernel, nz),
        out_shape=jax.ShapeDtypeStruct(expression.shape, jnp.bfloat16),
        in_specs=[any_spec] * 3,
        out_specs=any_spec,
        scratch_shapes=[
            pltpu.VMEM((shards * BLK + 1, BL, BL), jnp.bfloat16),
            pltpu.VMEM((shards * BLK + 1, BL, BL), jnp.bfloat16),
            pltpu.VMEM((NX, BLK, BL, BL), jnp.bfloat16),
            pltpu.VMEM((NX, BLK, SLOTS, BL, BL), jnp.bfloat16),
            pltpu.VMEM((NX, BLK, BL), jnp.int32),
            pltpu.SMEM((NX, BLK, BL), jnp.int32),
            dma((3,)),
            dma((3,)), dma((3,)),
            dma((3,)), dma((3,)),
            dma((2, 2)), dma((2, 2)),
            dma((2,)), dma((2,)),
            dma((2, 3)), dma((2, 3)),
            dma((2, 2, flow_len)), dma((2, 2, flow_len)),
            dma((2, 4 + 2 * flow_len)), dma((2, 4 + 2 * flow_len)),
            dma((3,)), dma((3,)),
        ],
        compiler_params=pltpu.CompilerParams(
            collective_id=0, has_side_effects=True, vmem_limit_bytes=56 * 2**20
        ),
    )(expression, affinity, lists)


def body(nz, expression, affinity, near_blocks, far_blocks, far_count):
    cell_rows = expression.shape[0]
    shard_total = nz * 2 * NX
    live = jnp.arange(far_blocks.shape[1], dtype=jnp.int32)[None, :] < far_count[:, None]
    far = jnp.where(live, far_blocks, shard_total * BLK)
    lists = jnp.concatenate([near_blocks, far], axis=1)
    lists = jnp.pad(lists, ((0, 0), (0, BL - SLOTS)))
    blocks = expression.reshape(BLK, BL, expression.shape[1])
    current = diffuse(blocks, affinity, lists, nz).reshape(expression.shape)
    whole = lax.all_gather(current, "genes", axis=1, tiled=True)
    summed = lax.psum_scatter(
        lax.dot_general(
            whole, current, (((0,), (0,)), ((), ())), preferred_element_type=jnp.float32
        ),
        "cells",
        scatter_dimension=0,
        tiled=True,
    )
    covariance = summed / (cell_rows * shard_total)
    return (current, covariance)


def solution(mesh):
    nz = mesh.shape["cells"] // (2 * NX)
    return jax.shard_map(
        functools.partial(body, nz),
        mesh=mesh,
        in_specs=(
            P("cells", "genes"),
            P("cells", None, None, None),
            P("cells", None),
            P("cells", None),
            P("cells"),
        ),
        out_specs=(P("cells", "genes"), P("cells", "genes")),
        check_vma=False,
    )
```

time: 667 us -> 417 us (0.63)
  waiting for transfers between devices: 552 us -> 187 us
  Pallas kernels: 0 us -> 197 us
  local copies, waits for them, and re-layouts: 36.8 us -> 2.33 us
  blocking collectives: 20 us -> 0 us
  starting transfers between devices: 13.8 us -> 0.08 us
  matrix products: 19.1 us -> 6.8 us
    all_to_all x2 -> x0, waiting for transfers between devices: 366 us -> none  [body(): lax.all_to_all(replies, 'cells', split_axis=0, concat_axis=0, tiled=True)]
    pallas_call x0 -> x1, Pallas kernels: none -> 197 us  [diffuse(): pl.pallas_call(functools.partial(diffuse_kernel, nz), out_shape=jax.Shape...]
    gather x6 -> x0, local copies, waits for them, and re-layouts: 34.7 us -> none  [the longest x2 18.1 us: body(): received[owners, ranks]]
    all_to_all x1 -> x0, blocking collectives: 20 us -> none  [body(): lax.all_to_all(table, 'cells', split_axis=0, concat_axis=0, tiled=True)]
    all_to_all x2 -> x0, starting transfers between devices: 13.5 us -> none  [body(): lax.all_to_all(replies, 'cells', split_axis=0, concat_axis=0, tiled=True)]
    dot_general x4 -> x0, matrix products: 12.2 us -> none  [the longest x2 9.66 us: body(): jnp.einsum('bkij,bkjg->big', far_weights, far_part, preferred_element_typ...]
  transfers between devices with their start and end apart: 4 -> 2, of which waited for: 4 -> 2; matrix products, arithmetic and copies ran while one was open for 1% -> 0% of each run, Pallas kernels for 0% -> 0%
where the time goes in v1:
time: 417 us; the launch traced here: 410 us
  Pallas kernels  197 us (47%)
  waiting for transfers between devices  187 us (45%)
  between operations  14 us (3%)
  matrix products  6.8 us (2%)
    pallas_call x1, Pallas kernels, diffuse(): pl.pallas_call(functools.partial(diffuse_kernel, nz), out_shape=jax.Shape...  197 us
    reduce_scatter x1, waiting for transfers between devices, body(): lax.psum_scatter(lax.dot_general(whole, current, (((0,), (0,)), ((), ()))...  138 us
    all_gather x1, waiting for transfers between devices, body(): whole = lax.all_gather(current, 'genes', axis=1, tiled=True)  48.8 us
  transfers between devices with their start and end apart: 2, of which 2 were waited for; matrix products, arithmetic and copies ran while one was open for 0% of the time, Pallas kernels for 0%

profile of v1, /device:TPU:33, one launch (start us, length us, event | category | flops | bytes accessed | tf_op | source)
XLA Modules:
  0.0 410.2 jit_solution(7938997423230338134)
XLA Ops:
  7.2 0.0 all-gather.2.cloned.1.call-start
  7.2 0.8 copy.7
  8.0 0.8 fusion
  8.7 0.1 pad_add_fusion
  8.8 0.6 pad.4.lists
  9.4 197.4 %shard_map.68 = bf16[8,128,512]{2,1,0:T(8,128)(2,1)} custom-call(bf16[8,128,512]{2,1,0:T(8,128)(2,1)} %bitcast.7, bf16[8,12,128,128]{3,2,1,0:T(8,128)(2,1)} %aff.1, s32[8,128]{1,0:T(8,128)} %pad.4.lists), custom_call_target="tpu_custom_call" | custom-call | tf_op jit(solution)/shard_map/pallas_call | solution.py:290
  206.8 0.0 all-gather.2.cloned.1.call-update
  206.8 0.0 reduce-scatter.2.cloned.1.call-start
  206.9 48.8 %all-gather.2.cloned.1.call-done = bf16[1024,2048]{1,0:T(8,128)(2,1)} async-done(((bf16[1024,512]{1,0:T(8,128)(2,1)}), bf16[1024,2048]{1,0:T(8,128)(2,1)}) %all-gather.2.cloned.1.call-update) | async-done | bytes 4194320 | tf_op jit(solution)/shard_map/all_gather | solution.py:327
  255.7 6.8 %fusion.1 = f32[2048,512]{1,0:T(8,128)} fusion(bf16[1024,2048]{1,0:T(8,128)(2,1)} %all-gather.2.cloned.1.call-done, bf16[1024,512]{1,0:T(8,128)(2,1)} %bitcast.5), kind=kOutput, calls=%fused_computation.4 | convolution fusion | flops 2147483648 | bytes 9437184 | tf_op jit(solution)/shard_map/dot_general | solution.py:329
  262.5 0.0 copy-start
  262.5 0.0 reduce-scatter.2.cloned.1.call-update
  262.5 138.4 %reduce-scatter.2.cloned.1.call-done = f32[32,512]{1,0:T(8,128)} async-done(((f32[2048,512]{1,0:T(8,128)}), f32[32,512]{1,0:T(8,128)}) %reduce-scatter.2.cloned.1.call-update) | async-done | bytes 65552 | tf_op jit(solution)/shard_map/reduce_scatter | solution.py:328
  400.9 1.5 broadcast_multiply_fusion
  402.4 0.0 copy-done
  402.4 1.0 copy.9
Async XLA Ops:
  7.2 248.5 %all-gather.2.cloned.1.call-start = ((), (), s32[]{:S(2)}) async-start(), calls=%async_computation.1 | async-start | bytes 5242880 | tf_op jit(solution)/shard_map/all_gather | solution.py:327
  206.8 194.0 %reduce-scatter.2.cloned.1.call-start = ((), (), s32[]{:S(2)}) async-start(), calls=%async_computation.2 | async-start | bytes 4259840 | tf_op jit(solution)/shard_map/reduce_scatter | solution.py:328
  262.5 139.9 %copy-start = (bf16[8,128,512]{2,1,0:T(8,128)(2,1)S(1)}, bf16[8,128,512]{2,1,0:T(8,128)(2,1)}, u32[]{:S(2)}) copy-start(bf16[8,128,512]{2,1,0:T(8,128)(2,1)} %shard_map.68) | copy-start | bytes 3145732
Sparse Core Ops, SparseCore 0:
  207.0 48.6 all-gather.1
  262.6 138.2 reduce-scatter.1

commit v2 on v1

--- a/solution.py
+++ b/solution.py
@@ -22,9 +22,9 @@
 
 
 def diffuse_kernel(
-    nz, expr, aff, lists, out, x0, x1, x2, w, lv, ls,
+    nz, scale, expr, aff, lists, out, cov, x0, x1, x2, w, lv, ls, s, st, gram, r1, r2, t, r3,
     loc, xs_s, xs_r, li_s, li_r, wx_s, wx_r, wf_s, wf_r, wy_s, wy_r,
-    z_s, z_r, p_s, p_r, o_s, o_r,
+    z_s, z_r, p_s, p_r, o_s, o_r, y_s, y_r, a_s, a_r, b_s, b_r, c_s, c_r,
 ):
     flow_len = 4 * (nz // 2) - 2
     me = lax.axis_index("cells")
@@ -43,14 +43,17 @@
     def x_dev(d):
         return (cell(z, wrap(x + d, NX), core), y)
 
-    right = (cell(wrap(z + 1, nz), x, core), y)
-    left = (cell(wrap(z - 1, nz), x, core), y)
+    def z_dev(d):
+        return (cell(wrap(z + d, nz), x, core), y)
+
+    right, left = z_dev(1), z_dev(nz - 1)
     partner = (cell(z, x, 1 - core), y)
     up = (me, wrap(y + 1, NY))
     down = (me, wrap(y - 1, NY))
 
     barrier = pltpu.get_barrier_semaphore()
-    peers = [x_dev(1), x_dev(2), x_dev(3), right, left, partner, up, down]
+    peers = [x_dev(d) for d in range(1, NX)] + [z_dev(d) for d in range(1, nz)]
+    peers += [partner, up, down]
     for peer in peers:
         pl.semaphore_signal(barrier, inc=1, device_id=peer, device_id_type=MESH)
     pl.semaphore_wait(barrier, len(peers))
@@ -247,7 +250,7 @@
 
     def give(j):
         return remote(
-            x2.at[j], columns(out, x), o_s.at[j - 1], o_r.at[j - 1],
+            x2.at[j], columns(s, x), o_s.at[j - 1], o_r.at[j - 1],
             (cell(z, wrap(x - j, NX), core), y),
         )
 
@@ -263,23 +266,119 @@
         def _():
             give(j).start()
 
-    own_out = pltpu.make_async_copy(x2.at[0], columns(out, x), loc.at[0])
+    def y_copy(way, n, p, j):
+        ref = st.at[p, wrap(x + j, NX)]
+        return remote(ref, ref, y_s.at[way, n], y_r.at[way, n], up if way == 0 else down)
+
+    def turn(j):
+        g = wrap(x + j, NX)
+        for b in range(BLK):
+            tile = s[b, :, pl.ds(pl.multiple_of(g * BL, BL), BL)]
+            st[y, g, :, pl.ds(b * BL, BL)] = tile.T
+        y_copy(0, j, y, j).start()
+        y_copy(1, j, y, j).start()
+
+    own_s = pltpu.make_async_copy(x2.at[0], columns(s, x), loc.at[0])
+    own_s.start()
+    own_s.wait()
+    turn(0)
+    for j in (1, 2, 3):
+        give(j).wait_recv()
+        turn(j)
+    own_out = pltpu.make_async_copy(s, out, loc.at[0])
     own_out.start()
+
+    def other_core(p, n):
+        return remote(
+            gram.at[pl.ds(2 * p, 2), :, 1 - core], r1.at[pl.ds(2 * p, 2)], a_s.at[n], a_r.at[n], partner
+        )
+
+    def along_x(p, n, d):
+        return remote(
+            r1.at[pl.ds(2 * p, 2), wrap(x + d, NX)], r2.at[d - 1, pl.ds(2 * p, 2)],
+            b_s.at[n, d - 1], b_r.at[n, d - 1], x_dev(d),
+        )
+
+    def along_z(d):
+        return remote(t.at[wrap(z + d, nz)], r3.at[d - 1], c_s.at[d - 1], c_r.at[d - 1], z_dev(d))
+
+    def panel(p, n):
+        @pl.loop(0, 4)
+        def _(g):
+            rows = jnp.dot(
+                st[p, g], s[...].reshape(BLK * BL, 4 * BL), preferred_element_type=jnp.float32
+            )
+            gram[2 * p + g // 2, pl.ds(2 * lax.rem(g, 2), 2)] = rows.reshape(2, 2, 32, 4 * BL)
+
+        other_core(p, n).start()
+
+    def panel_x(p, n):
+        other_core(p, n).wait_recv()
+        for i in range(2):
+            for xx in range(NX):
+                r1[2 * p + i, xx] += gram[2 * p + i, xx, core]
+        for d in (1, 3, 2):
+            along_x(p, n, d).start()
+
+    def panel_sum(p, n):
+        for d in (1, 3, 2):
+            along_x(p, n, d).wait_recv()
+        for i in range(2):
+            k = 2 * p + i
+            t[k] = (r1[k, x] + r2[0, k]) + (r2[1, k] + r2[2, k])
+
+    order = [y, wrap(y - 1, NY), wrap(y + 1, NY), wrap(y + 2, NY)]
+    panel(order[0], 0)
+    for j in range(4):
+        y_copy(0, j, order[1], j).wait_recv()
+        if j < 2:
+            y_copy(0, 4 + j, order[1], j).start()
+        y_copy(1, j, order[2], j).wait_recv()
+        if j >= 2:
+            y_copy(1, 2 + j, order[2], j).start()
+    panel(order[1], 1)
+    panel(order[2], 2)
+    panel_x(order[0], 0)
+    panel_x(order[1], 1)
+    panel_x(order[2], 2)
+    panel_sum(order[0], 0)
+    for j in range(2):
+        y_copy(0, 4 + j, order[3], j).wait_recv()
+        y_copy(1, 4 + j, order[3], 2 + j).wait_recv()
+    panel(order[3], 3)
+    panel_sum(order[1], 1)
+    panel_sum(order[2], 2)
+    panel_x(order[3], 3)
+    panel_sum(order[3], 3)
+    for d in range(1, nz):
+        along_z(d).start()
+    total = t[z]
+    for d in range(1, nz):
+        along_z(d).wait_recv()
+        total += r3[d - 1]
+    cov[...] = total * scale
 
     for d in (1, 2, 3):
         deal(d).wait_send()
         names(d).wait_send()
+        give(d).wait_send()
         for u in range(2):
             w_across(d - 1, u).wait_send()
     for way in range(2):
         w_forward(way).wait_send()
         for u in range(2):
             w_first(way, u).wait_send()
+        for n in range(6):
+            y_copy(way, n, y, 0).wait_send()
     sends_done(0, x0)
     sends_done(1, x1)
+    for n in range(4):
+        other_core(y, n).wait_send()
+        for d in (1, 2, 3):
+            along_x(y, n, d).wait_send()
+    for d in range(1, nz):
+        along_z(d).wait_send()
     own_out.wait()
-    for j in (1, 2, 3):
-        give(j).wait()
 
 
 def diffuse(expression, affinity, lists, nz):
@@ -288,10 +387,13 @@
     dma = pltpu.SemaphoreType.DMA
     any_spec = pl.BlockSpec(memory_space=pl.ANY)
     return pl.pallas_call(
-        functools.partial(diffuse_kernel, nz),
-        out_shape=jax.ShapeDtypeStruct(expression.shape, jnp.bfloat16),
+        functools.partial(diffuse_kernel, nz, 1.0 / (shards * BLK * BL)),
+        out_shape=(
+            jax.ShapeDtypeStruct(expression.shape, jnp.bfloat16),
+            jax.ShapeDtypeStruct((32, NX * BL), jnp.float32),
+        ),
         in_specs=[any_spec] * 3,
-        out_specs=any_spec,
+        out_specs=(any_spec, pl.BlockSpec(memory_space=pltpu.VMEM)),
         scratch_shapes=[
             pltpu.VMEM((shards * BLK + 1, BL, BL), jnp.bfloat16),
             pltpu.VMEM((shards * BLK + 1, BL, BL), jnp.bfloat16),
@@ -299,6 +401,13 @@
             pltpu.VMEM((NX, BLK, SLOTS, BL, BL), jnp.bfloat16),
             pltpu.VMEM((NX, BLK, BL), jnp.int32),
             pltpu.SMEM((NX, BLK, BL), jnp.int32),
+            pltpu.VMEM((BLK, BL, NX * BL), jnp.bfloat16),
+            pltpu.VMEM((NY, NX, BL, BLK * BL), jnp.bfloat16),
+            pltpu.VMEM((nz, NX, 2, 32, NX * BL), jnp.float32),
+            pltpu.VMEM((nz, NX, 32, NX * BL), jnp.float32),
+            pltpu.VMEM((NX - 1, nz, 32, NX * BL), jnp.float32),
+            pltpu.VMEM((nz, 32, NX * BL), jnp.float32),
+            pltpu.VMEM((nz - 1, 32, NX * BL), jnp.float32),
             dma((3,)),
             dma((3,)), dma((3,)),
             dma((3,)), dma((3,)),
@@ -308,33 +417,26 @@
             dma((2, 2, flow_len)), dma((2, 2, flow_len)),
             dma((2, 4 + 2 * flow_len)), dma((2, 4 + 2 * flow_len)),
             dma((3,)), dma((3,)),
+            dma((2, 6)), dma((2, 6)),
+            dma((NY,)), dma((NY,)),
+            dma((NY, NX - 1)), dma((NY, NX - 1)),
+            dma((nz - 1,)), dma((nz - 1,)),
         ],
         compiler_params=pltpu.CompilerParams(
-            collective_id=0, has_side_effects=True, vmem_limit_bytes=56 * 2**20
+            collective_id=0, has_side_effects=True, vmem_limit_bytes=61 * 2**20
         ),
     )(expression, affinity, lists)
 
 
 def body(nz, expression, affinity, near_blocks, far_blocks, far_count):
-    cell_rows = expression.shape[0]
     shard_total = nz * 2 * NX
     live = jnp.arange(far_blocks.shape[1], dtype=jnp.int32)[None, :] < far_count[:, None]
     far = jnp.where(live, far_blocks, shard_total * BLK)
     lists = jnp.concatenate([near_blocks, far], axis=1)
     lists = jnp.pad(lists, ((0, 0), (0, BL - SLOTS)))
     blocks = expression.reshape(BLK, BL, expression.shape[1])
-    current = diffuse(blocks, affinity, lists, nz).reshape(expression.shape)
-    whole = lax.all_gather(current, "genes", axis=1, tiled=True)
-    summed = lax.psum_scatter(
-        lax.dot_general(
-            whole, current, (((0,), (0,)), ((), ())), preferred_element_type=jnp.float32
-        ),
-        "cells",
-        scatter_dimension=0,
-        tiled=True,
-    )
-    covariance = summed / (cell_rows * shard_total)
-    return (current, covariance)
+    current, covariance = diffuse(blocks, affinity, lists, nz)
+    return (current.reshape(expression.shape), covariance)
 
 
 def solution(mesh):

time: 417 us -> 267 us (0.64); the launches traced: 410 us -> 266 us
  waiting for transfers between devices: 187 us -> 0 us
  Pallas kernels: 197 us -> 259 us
  between operations: 14 us -> 0.64 us
  matrix products: 6.8 us -> 0 us
    reduce_scatter x1 -> x0, waiting for transfers between devices: 138 us -> none  [body(): lax.psum_scatter(lax.dot_general(whole, current, (((0,), (0,)), ((), ()))...]
    pallas_call x1, Pallas kernels: 197 us -> 259 us  [diffuse(): pl.pallas_call(functools.partial(diffuse_kernel, nz, 1.0 / (shards * BLK...]
    all_gather x1 -> x0, waiting for transfers between devices: 48.8 us -> none  [body(): whole = lax.all_gather(current, 'genes', axis=1, tiled=True)]
    dot_general x1 -> x0, matrix products: 6.8 us -> none  [body(): lax.dot_general(whole, current, (((0,), (0,)), ((), ())), preferred_eleme...]
  transfers between devices with their start and end apart: 2 -> 0, of which waited for: 2 -> 0; matrix products, arithmetic and copies ran while one was open for 0% -> 0% of each run, Pallas kernels for 0% -> 0%
where the time goes in v2:
time: 267 us; the launch traced here: 266 us
  Pallas kernels  259 us (97%)
  local copies, waits for them, and re-layouts  5.09 us (2%)
    pallas_call x1, Pallas kernels, diffuse(): pl.pallas_call(functools.partial(diffuse_kernel, nz, 1.0 / (shards * BLK...  259 us

profile of v2, /device:TPU:33, one launch (start us, length us, event | category | flops | bytes accessed | tf_op | source)
XLA Modules:
  0.0 265.5 jit_solution(16395746402622477371)
XLA Ops:
  0.6 0.8 copy.7
  1.4 0.8 fusion
  2.1 0.1 pad_add_fusion
  2.2 0.6 pad.4.lists
  2.8 259.0 %shard_map.68 = (bf16[8,128,512]{2,1,0:T(8,128)(2,1)}, f32[32,512]{1,0:T(8,128)}) custom-call(bf16[8,128,512]{2,1,0:T(8,128)(2,1)} %bitcast.2, bf16[8,12,128,128]{3,2,1,0:T(8,128)(2,1)} %aff.1, s32[8,128]{1,0:T(8,128)} %pad.4.lists), custom_call_target="tpu_custom_call" | custom-call | tf_op jit(solution)/shard_map/pallas_call | solution.py:389
  261.8 2.3 copy.10
  264.1 1.5 copy.11

commit v3 on v1

--- a/solution.py
+++ b/solution.py
@@ -22,9 +22,9 @@
 
 
 def diffuse_kernel(
-    nz, expr, aff, lists, out, x0, x1, x2, w, lv, ls,
+    nz, scale, expr, aff, lists, out, cov, x0, x1, w, lv, ls, sx, st, gram, r1, r3,
     loc, xs_s, xs_r, li_s, li_r, wx_s, wx_r, wf_s, wf_r, wy_s, wy_r,
-    z_s, z_r, p_s, p_r, o_s, o_r,
+    z_s, z_r, p_s, p_r, g_s, g_r, a_s, a_r, c_s, c_r,
 ):
     flow_len = 4 * (nz // 2) - 2
     me = lax.axis_index("cells")
@@ -49,11 +49,21 @@
     up = (me, wrap(y + 1, NY))
     down = (me, wrap(y - 1, NY))
 
+    def sink(n):
+        return cell(2 * (n // 2) + x // 2, 2 * lax.rem(x, 2) + n % 2, core)
+
+    def source(zz):
+        return cell(zz, 2 * lax.rem(z, 2) + x // 2, core)
+
     barrier = pltpu.get_barrier_semaphore()
     peers = [x_dev(1), x_dev(2), x_dev(3), right, left, partner, up, down]
     for peer in peers:
         pl.semaphore_signal(barrier, inc=1, device_id=peer, device_id_type=MESH)
-    pl.semaphore_wait(barrier, len(peers))
+    for zz in range(nz):
+        @pl.when(source(zz) != me)
+        def _():
+            pl.semaphore_signal(barrier, inc=1, device_id=(source(zz), y), device_id_type=MESH)
+    pl.semaphore_wait(barrier, len(peers) + nz - jnp.where(source(z) == me, 1, 0))
 
     def piece(buf, shard):
         return buf.at[pl.ds(shard * BLK, BLK)]
@@ -245,26 +255,107 @@
     pass_on(1, x1, 0, flow_len)
     partner_done(1, x1)
 
-    def give(j):
-        return remote(
-            x2.at[j], columns(out, x), o_s.at[j - 1], o_r.at[j - 1],
-            (cell(z, wrap(x - j, NX), core), y),
-        )
+    def turn_x(way, n, xt, xc):
+        ref = sx.at[xt, xc]
+        return remote(ref, ref, g_s.at[0, way, n], g_r.at[0, way, n], x_dev(1 if way == 0 else 3))
+
+    def turn_y(way, n, yt, xc):
+        ref = st.at[yt, xc]
+        return remote(ref, ref, g_s.at[1, way, n], g_r.at[1, way, n], up if way == 0 else down)
 
     @pl.loop(0, NX)
     def _(j):
-        xs = wrap(x - j, NX)
+        xc = wrap(x - j, NX)
 
         @pl.loop(0, BLK)
         def _(b):
-            x2[j, b] = block_sum(x1, xs, b)
-
-        @pl.when(j > 0)
+            value = block_sum(x1, xc, b)
+            sx[x, xc, b] = value
+            st[y, xc, :, pl.ds(pl.multiple_of(b * BL, BL), BL)] = value.T
+
+        for way in range(2):
+            turn_x(way, j, x, xc).start()
+            turn_y(way, j, y, xc).start()
+
+    xl, xr, xo = wrap(x - 1, NX), wrap(x + 1, NX), wrap(x + 2, NX)
+    yd, yu, yo = wrap(y - 1, NY), wrap(y + 1, NY), wrap(y + 2, NY)
+    for j in range(NX):
+        turn_x(0, j, xl, wrap(xl - j, NX)).wait_recv()
+        turn_y(0, j, yd, wrap(x - j, NX)).wait_recv()
+        if j < 2:
+            turn_x(0, 4 + j, xl, wrap(xl - j, NX)).start()
+            turn_y(0, 4 + j, yd, wrap(x - j, NX)).start()
+        turn_x(1, j, xr, wrap(xr - j, NX)).wait_recv()
+        turn_y(1, j, yu, wrap(x - j, NX)).wait_recv()
+        if j >= 2:
+            turn_x(1, 2 + j, xr, wrap(xr - j, NX)).start()
+            turn_y(1, 2 + j, yu, wrap(x - j, NX)).start()
+
+    def product(yts, xts):
+        @pl.loop(0, NX)
+        def _(xc):
+            lhs = jnp.concatenate([st[yt, xc] for yt in yts], axis=0)
+            rhs = jnp.concatenate(
+                [sx[xt, xc].reshape(BLK * BL, BL) for xt in xts], axis=1
+            )
+            part = jnp.dot(lhs, rhs, preferred_element_type=jnp.float32)
+            for i, yt in enumerate(yts):
+                for k, xt in enumerate(xts):
+                    cols = pl.ds(pl.multiple_of(xt * BL, BL), BL)
+                    tile = part[i * BL:(i + 1) * BL, k * BL:(k + 1) * BL].reshape(2, 2, 32, BL)
+
+                    @pl.when(xc == 0)
+                    def _():
+                        gram[yt, :, :, :, cols] = tile
+
+                    @pl.when(xc > 0)
+                    def _():
+                        gram[yt, :, :, :, cols] += tile
+
+    product([y, yd, yu], [x, xl])
+    product([y, yd, yu], [xr])
+    for j in range(2):
+        turn_x(0, 4 + j, xo, wrap(xo - j, NX)).wait_recv()
+        turn_y(0, 4 + j, yo, wrap(x - j, NX)).wait_recv()
+        turn_x(1, 4 + j, xo, wrap(xo - 2 - j, NX)).wait_recv()
+        turn_y(1, 4 + j, yo, wrap(x - 2 - j, NX)).wait_recv()
+    product([y, yd, yu], [xo])
+    product([yo], [x, xl])
+    product([yo], [xr, xo])
+
+    other = remote(gram.at[:, :, 1 - core], r1, a_s.at[0], a_r.at[0], partner)
+    other.start()
+
+    def write_out(xt):
+        return pltpu.make_async_copy(sx.at[xt, x], columns(out, xt), loc.at[xt])
+
+    for xt in range(NX):
+        write_out(xt).start()
+
+    def to_owner(n):
+        return remote(r1.at[n // 2, n % 2], r3.at[z], c_s.at[n], c_r.at[z], (sink(n), y))
+
+    other.wait_recv()
+    for n in range(nz):
+        r1[n // 2, n % 2] += gram[n // 2, n % 2, core]
+
+        @pl.when(sink(n) != me)
         def _():
-            give(j).start()
-
-    own_out = pltpu.make_async_copy(x2.at[0], columns(out, x), loc.at[0])
-    own_out.start()
+            to_owner(n).start()
+
+    @pl.when(source(z) == me)
+    def _():
+        r3[z] = r1[z // 2, lax.rem(x, 2)]
+
+    for zz in range(nz):
+        @pl.when(source(zz) != me)
+        def _():
+            remote(r1.at[0, 0], r3.at[zz], c_s.at[0], c_r.at[zz], (source(zz), y)).wait_recv()
+
+    total = r3[0]
+    for zz in range(1, nz):
+        total += r3[zz]
+    cov[...] = total * scale
 
     for d in (1, 2, 3):
         deal(d).wait_send()
@@ -275,11 +366,18 @@
         w_forward(way).wait_send()
         for u in range(2):
             w_first(way, u).wait_send()
+        for n in range(6):
+            turn_x(way, n, x, x).wait_send()
+            turn_y(way, n, y, x).wait_send()
     sends_done(0, x0)
     sends_done(1, x1)
-    own_out.wait()
-    for j in (1, 2, 3):
-        give(j).wait()
+    other.wait_send()
+    for n in range(nz):
+        @pl.when(sink(n) != me)
+        def _():
+            to_owner(n).wait_send()
+    for xt in range(NX):
+        write_out(xt).wait()
 
 
 def diffuse(expression, affinity, lists, nz):
@@ -288,18 +386,25 @@
     dma = pltpu.SemaphoreType.DMA
     any_spec = pl.BlockSpec(memory_space=pl.ANY)
     return pl.pallas_call(
-        functools.partial(diffuse_kernel, nz),
-        out_shape=jax.ShapeDtypeStruct(expression.shape, jnp.bfloat16),
+        functools.partial(diffuse_kernel, nz, 1.0 / (shards * BLK * BL)),
+        out_shape=(
+            jax.ShapeDtypeStruct(expression.shape, jnp.bfloat16),
+            jax.ShapeDtypeStruct((32, NX * BL), jnp.float32),
+        ),
         in_specs=[any_spec] * 3,
-        out_specs=any_spec,
+        out_specs=(any_spec, pl.BlockSpec(memory_space=pltpu.VMEM)),
         scratch_shapes=[
             pltpu.VMEM((shards * BLK + 1, BL, BL), jnp.bfloat16),
             pltpu.VMEM((shards * BLK + 1, BL, BL), jnp.bfloat16),
-            pltpu.VMEM((NX, BLK, BL, BL), jnp.bfloat16),
             pltpu.VMEM((NX, BLK, SLOTS, BL, BL), jnp.bfloat16),
             pltpu.VMEM((NX, BLK, BL), jnp.int32),
             pltpu.SMEM((NX, BLK, BL), jnp.int32),
-            dma((3,)),
+            pltpu.VMEM((NX, NX, BLK, BL, BL), jnp.bfloat16),
+            pltpu.VMEM((NY, NX, BL, BLK * BL), jnp.bfloat16),
+            pltpu.VMEM((NY, 2, 2, 32, NX * BL), jnp.float32),
+            pltpu.VMEM((NY, 2, 32, NX * BL), jnp.float32),
+            pltpu.VMEM((nz, 32, NX * BL), jnp.float32),
+            dma((4,)),
             dma((3,)), dma((3,)),
             dma((3,)), dma((3,)),
             dma((2, 2)), dma((2, 2)),
@@ -307,34 +412,25 @@
             dma((2, 3)), dma((2, 3)),
             dma((2, 2, flow_len)), dma((2, 2, flow_len)),
             dma((2, 4 + 2 * flow_len)), dma((2, 4 + 2 * flow_len)),
-            dma((3,)), dma((3,)),
+            dma((2, 2, 6)), dma((2, 2, 6)),
+            dma((1,)), dma((1,)),
+            dma((nz,)), dma((nz,)),
         ],
         compiler_params=pltpu.CompilerParams(
-            collective_id=0, has_side_effects=True, vmem_limit_bytes=56 * 2**20
+            collective_id=0, has_side_effects=True, vmem_limit_bytes=60 * 2**20
         ),
     )(expression, affinity, lists)
 
 
 def body(nz, expression, affinity, near_blocks, far_blocks, far_count):
-    cell_rows = expression.shape[0]
     shard_total = nz * 2 * NX
     live = jnp.arange(far_blocks.shape[1], dtype=jnp.int32)[None, :] < far_count[:, None]
     far = jnp.where(live, far_blocks, shard_total * BLK)
     lists = jnp.concatenate([near_blocks, far], axis=1)
     lists = jnp.pad(lists, ((0, 0), (0, BL - SLOTS)))
     blocks = expression.reshape(BLK, BL, expression.shape[1])
-    current = diffuse(blocks, affinity, lists, nz).reshape(expression.shape)
-    whole = lax.all_gather(current, "genes", axis=1, tiled=True)
-    summed = lax.psum_scatter(
-        lax.dot_general(
-            whole, current, (((0,), (0,)), ((), ())), preferred_element_type=jnp.float32
-        ),
-        "cells",
-        scatter_dimension=0,
-        tiled=True,
-    )
-    covariance = summed / (cell_rows * shard_total)
-    return (current, covariance)
+    current, covariance = diffuse(blocks, affinity, lists, nz)
+    return (current.reshape(expression.shape), covariance)
 
 
 def solution(mesh):

time: 417 us -> 256 us (0.61)
  waiting for transfers between devices: 187 us -> 0 us
  Pallas kernels: 197 us -> 245 us
  between operations: 14 us -> 0.64 us
  matrix products: 6.8 us -> 0 us
    reduce_scatter x1 -> x0, waiting for transfers between devices: 138 us -> none  [body(): lax.psum_scatter(lax.dot_general(whole, current, (((0,), (0,)), ((), ()))...]
    all_gather x1 -> x0, waiting for transfers between devices: 48.8 us -> none  [body(): whole = lax.all_gather(current, 'genes', axis=1, tiled=True)]
    pallas_call x1, Pallas kernels: 197 us -> 245 us  [diffuse(): pl.pallas_call(functools.partial(diffuse_kernel, nz, 1.0 / (shards * BLK...]
    dot_general x1 -> x0, matrix products: 6.8 us -> none  [body(): lax.dot_general(whole, current, (((0,), (0,)), ((), ())), preferred_eleme...]
  transfers between devices with their start and end apart: 2 -> 0, of which waited for: 2 -> 0; matrix products, arithmetic and copies ran while one was open for 0% -> 0% of each run, Pallas kernels for 0% -> 0%
where the time goes in v3:
time: 256 us; the launch traced here: 252 us
  Pallas kernels  245 us (96%)
  local copies, waits for them, and re-layouts  5.09 us (2%)
    pallas_call x1, Pallas kernels, diffuse(): pl.pallas_call(functools.partial(diffuse_kernel, nz, 1.0 / (shards * BLK...  245 us

profile of v3, /device:TPU:33, one launch (start us, length us, event | category | flops | bytes accessed | tf_op | source)
XLA Modules:
  0.0 252.0 jit_solution(16023519090867206151)
XLA Ops:
  0.6 0.8 copy.7
  1.4 0.8 fusion
  2.1 0.1 pad_add_fusion
  2.2 0.6 pad.4.lists
  2.8 245.4 %shard_map.68 = (bf16[8,128,512]{2,1,0:T(8,128)(2,1)}, f32[32,512]{1,0:T(8,128)}) custom-call(bf16[8,128,512]{2,1,0:T(8,128)(2,1)} %bitcast.2, bf16[8,12,128,128]{3,2,1,0:T(8,128)(2,1)} %aff.1, s32[8,128]{1,0:T(8,128)} %pad.4.lists), custom_call_target="tpu_custom_call" | custom-call | tf_op jit(solution)/shard_map/pallas_call | solution.py:388
  248.2 2.3 copy.10
  250.5 1.5 copy.11

commit v4 on v3

--- a/solution.py
+++ b/solution.py
@@ -13,6 +13,7 @@
 BL = 128
 BLK = 8
 SLOTS = 12
+LOC = 4
 
 
 def remote(src, dst, send, recv, device):
@@ -22,7 +23,7 @@
 
 
 def diffuse_kernel(
-    nz, scale, expr, aff, lists, out, cov, x0, x1, w, lv, ls, sx, st, gram, r1, r3,
+    nz, scale, expr, aff, near, far, count, out, cov, x0, x1, w, lv, ls, sx, st, gram, r1, rz, r3,
     loc, xs_s, xs_r, li_s, li_r, wx_s, wx_r, wf_s, wf_r, wy_s, wy_r,
     z_s, z_r, p_s, p_r, g_s, g_r, a_s, a_r, c_s, c_r,
 ):
@@ -81,55 +82,56 @@
     for d in (1, 3, 2):
         deal(d).start()
 
+    slot = lax.broadcasted_iota(jnp.int32, (1, BLK), 1)
+    for b in range(BLK):
+        lv[x, b:b + 1, 0:BLK] = jnp.where(slot < count[b], far[b:b + 1, :], nz * 2 * NX * BLK)
+    lv[x, BLK:BLK + LOC, 0:BLK] = near[...]
+
     def names(d):
-        return remote(lists, lv.at[x], li_s.at[d - 1], li_r.at[d - 1], x_dev(d))
-
-    own_names = pltpu.make_async_copy(lists, lv.at[x], loc.at[1])
-    own_names.start()
+        return remote(lv.at[x], lv.at[x], li_s.at[d - 1], li_r.at[d - 1], x_dev(d))
+
     for d in (1, 2, 3):
         names(d).start()
 
     own_w = pltpu.make_async_copy(aff, w.at[x], loc.at[2])
 
-    def wsub(xx, hh, u):
-        return w.at[xx, pl.ds(4 * hh + 2 * u, 2)]
-
-    def w_first(way, u):
+    def wsub(xx, hh, i):
+        return w.at[xx, 4 * hh + i]
+
+    def w_first(way, n):
+        i = n if way == 0 else 3 - n
         return remote(
-            aff.at[pl.ds(4 * half + 2 * u, 2)], wsub(x, half, u),
-            wx_s.at[way, u], wx_r.at[way, u], x_dev(1 if way == 0 else 3),
+            aff.at[4 * half + i], wsub(x, half, i), wx_s.at[way, n], wx_r.at[way, n],
+            x_dev(1 if way == 0 else 3),
         )
 
-    def w_forward(way):
-        ref = wsub(wrap(x - 1, NX), half, 0) if way == 0 else wsub(wrap(x + 1, NX), half, 1)
-        return remote(ref, ref, wf_s.at[way], wf_r.at[way], x_dev(1 if way == 0 else 3))
-
-    def w_across(e, u):
-        ref = wsub(wrap(x + (3, 1, 2)[e], NX), half, u)
-        return remote(ref, ref, wy_s.at[u, e], wy_r.at[u, e], up if u == 0 else down)
-
-    for way, u in ((0, 0), (1, 1), (0, 1), (1, 0)):
-        w_first(way, u).start()
+    def w_forward(way, n):
+        i = n if way == 0 else 3 - n
+        ref = wsub(wrap(x - 1, NX) if way == 0 else wrap(x + 1, NX), half, i)
+        return remote(ref, ref, wf_s.at[way, n], wf_r.at[way, n], x_dev(1 if way == 0 else 3))
+
+    def w_across(e, i):
+        ref = wsub(wrap(x + (3, 1, 2)[e], NX), half, i)
+        return remote(ref, ref, wy_s.at[e, i], wy_r.at[e, i], up if i < 2 else down)
+
+    for n in range(2):
+        w_first(0, n).start()
+        w_first(1, n).start()
     own_w.start()
 
-    def w_serve(stage):
-        if stage == 0:
-            w_first(0, 0).wait_recv()
-            w_forward(0).start()
-            w_across(0, 0).start()
-            w_first(1, 1).wait_recv()
-            w_forward(1).start()
-            w_across(1, 1).start()
-        elif stage == 1:
-            w_first(0, 1).wait_recv()
-            w_across(0, 1).start()
-            w_first(1, 0).wait_recv()
-            w_across(1, 0).start()
-        else:
-            w_forward(0).wait_recv()
-            w_across(2, 0).start()
-            w_forward(1).wait_recv()
-            w_across(2, 1).start()
+    def w_serve(n):
+        for way in range(2):
+            i = n % 4 if way == 0 else 3 - n % 4
+            if n < 4:
+                w_first(way, n).wait_recv()
+                if n < 2:
+                    w_forward(way, n).start()
+                w_across(way, i).start()
+                if n < 2:
+                    w_first(way, n + 2).start()
+            else:
+                w_forward(way, n - 4).wait_recv()
+                w_across(2, i).start()
 
     def shard_of(zz, j, kk):
         return cell(wrap(zz, nz), wrap(x - j, NX), kk)
@@ -202,10 +204,13 @@
         def _(q):
             p_copy(n, buf, q, shard).wait_send()
 
+    def name(xs, b, slot):
+        return ls[xs, BLK + slot, b] if slot < LOC else ls[xs, b, slot - LOC]
+
     def block_sum(buf, xs, b):
         total = None
         for pair in range(SLOTS // 2):
-            rows = [buf[ls[xs, b, 2 * pair + i]] for i in range(2)]
+            rows = [buf[name(xs, b, 2 * pair + i)] for i in range(2)]
             mats = [w[xs, b, 2 * pair + i] for i in range(2)]
             term = jnp.dot(
                 jnp.concatenate(mats, axis=1), jnp.concatenate(rows, axis=0),
@@ -223,13 +228,12 @@
     for j in (1, 3, 2):
         deal(j).wait_recv()
         send_own(0, x0, j)
-    cuts = (0, flow_len // 2 - 1, flow_len // 2 + 2, flow_len - 1, flow_len)
-    for part in range(4):
+    cuts = (0, 3, 4, 6, 7, 8, 9, flow_len)
+    for part in range(7):
         pass_on(0, x0, cuts[part], cuts[part + 1])
-        if part < 3:
+        if part < 6:
             w_serve(part)
 
-    own_names.wait()
     for d in (1, 2, 3):
         names(d).wait_recv()
     to_smem = pltpu.make_async_copy(lv, ls, loc.at[1])
@@ -238,8 +242,8 @@
     own_w.wait()
     partner_done(0, x0)
     for e in range(3):
-        for u in range(2):
-            w_across(e, u).wait_recv()
+        for i in range(4):
+            w_across(e, i).wait_recv()
 
     @pl.loop(0, NX)
     def _(j):
@@ -333,11 +337,12 @@
         write_out(xt).start()
 
     def to_owner(n):
-        return remote(r1.at[n // 2, n % 2], r3.at[z], c_s.at[n], c_r.at[z], (sink(n), y))
+        return remote(rz.at[n // 2, n % 2], r3.at[z], c_s.at[n], c_r.at[z], (sink(n), y))
 
     other.wait_recv()
     for n in range(nz):
-        r1[n // 2, n % 2] += gram[n // 2, n % 2, core]
+        both = r1[n // 2, n % 2] + gram[n // 2, n % 2, core]
+        rz[n // 2, n % 2] = both.astype(jnp.bfloat16)
 
         @pl.when(sink(n) != me)
         def _():
@@ -345,27 +350,28 @@
 
     @pl.when(source(z) == me)
     def _():
-        r3[z] = r1[z // 2, lax.rem(x, 2)]
+        r3[z] = rz[z // 2, lax.rem(x, 2)]
 
     for zz in range(nz):
         @pl.when(source(zz) != me)
         def _():
-            remote(r1.at[0, 0], r3.at[zz], c_s.at[0], c_r.at[zz], (source(zz), y)).wait_recv()
-
-    total = r3[0]
+            remote(rz.at[0, 0], r3.at[zz], c_s.at[0], c_r.at[zz], (source(zz), y)).wait_recv()
+
+    total = r3[0].astype(jnp.float32)
     for zz in range(1, nz):
-        total += r3[zz]
+        total += r3[zz].astype(jnp.float32)
     cov[...] = total * scale
 
     for d in (1, 2, 3):
         deal(d).wait_send()
         names(d).wait_send()
-        for u in range(2):
-            w_across(d - 1, u).wait_send()
+        for i in range(4):
+            w_across(d - 1, i).wait_send()
     for way in range(2):
-        w_forward(way).wait_send()
-        for u in range(2):
-            w_first(way, u).wait_send()
+        for n in range(2):
+            w_forward(way, n).wait_send()
+        for n in range(4):
+            w_first(way, n).wait_send()
         for n in range(6):
             turn_x(way, n, x, x).wait_send()
             turn_y(way, n, y, x).wait_send()
@@ -380,7 +386,7 @@
         write_out(xt).wait()
 
 
-def diffuse(expression, affinity, lists, nz):
+def diffuse(expression, affinity, near, far, count, nz):
     shards = nz * 2 * NX
     flow_len = 4 * (nz // 2) - 2
     dma = pltpu.SemaphoreType.DMA
@@ -391,25 +397,32 @@
             jax.ShapeDtypeStruct(expression.shape, jnp.bfloat16),
             jax.ShapeDtypeStruct((32, NX * BL), jnp.float32),
         ),
-        in_specs=[any_spec] * 3,
+        in_specs=[
+            any_spec,
+            any_spec,
+            pl.BlockSpec(memory_space=pltpu.VMEM),
+            pl.BlockSpec(memory_space=pltpu.VMEM),
+            pl.BlockSpec(memory_space=pltpu.SMEM),
+        ],
         out_specs=(any_spec, pl.BlockSpec(memory_space=pltpu.VMEM)),
         scratch_shapes=[
             pltpu.VMEM((shards * BLK + 1, BL, BL), jnp.bfloat16),
             pltpu.VMEM((shards * BLK + 1, BL, BL), jnp.bfloat16),
             pltpu.VMEM((NX, BLK, SLOTS, BL, BL), jnp.bfloat16),
-            pltpu.VMEM((NX, BLK, BL), jnp.int32),
-            pltpu.SMEM((NX, BLK, BL), jnp.int32),
+            pltpu.VMEM((NX, 2 * BLK, BL), jnp.int32),
+            pltpu.SMEM((NX, 2 * BLK, BL), jnp.int32),
             pltpu.VMEM((NX, NX, BLK, BL, BL), jnp.bfloat16),
             pltpu.VMEM((NY, NX, BL, BLK * BL), jnp.bfloat16),
             pltpu.VMEM((NY, 2, 2, 32, NX * BL), jnp.float32),
             pltpu.VMEM((NY, 2, 32, NX * BL), jnp.float32),
-            pltpu.VMEM((nz, 32, NX * BL), jnp.float32),
+            pltpu.VMEM((NY, 2, 32, NX * BL), jnp.bfloat16),
+            pltpu.VMEM((nz, 32, NX * BL), jnp.bfloat16),
             dma((4,)),
             dma((3,)), dma((3,)),
             dma((3,)), dma((3,)),
+            dma((2, 4)), dma((2, 4)),
             dma((2, 2)), dma((2, 2)),
-            dma((2,)), dma((2,)),
-            dma((2, 3)), dma((2, 3)),
+            dma((3, 4)), dma((3, 4)),
             dma((2, 2, flow_len)), dma((2, 2, flow_len)),
             dma((2, 4 + 2 * flow_len)), dma((2, 4 + 2 * flow_len)),
             dma((2, 2, 6)), dma((2, 2, 6)),
@@ -419,17 +432,14 @@
         compiler_params=pltpu.CompilerParams(
             collective_id=0, has_side_effects=True, vmem_limit_bytes=60 * 2**20
         ),
-    )(expression, affinity, lists)
+    )(expression, affinity, near, far, count)
 
 
 def body(nz, expression, affinity, near_blocks, far_blocks, far_count):
-    shard_total = nz * 2 * NX
-    live = jnp.arange(far_blocks.shape[1], dtype=jnp.int32)[None, :] < far_count[:, None]
-    far = jnp.where(live, far_blocks, shard_total * BLK)
-    lists = jnp.concatenate([near_blocks, far], axis=1)
-    lists = jnp.pad(lists, ((0, 0), (0, BL - SLOTS)))
     blocks = expression.reshape(BLK, BL, expression.shape[1])
-    current, covariance = diffuse(blocks, affinity, lists, nz)
+    current, covariance = diffuse(
+        blocks, affinity, near_blocks.T, far_blocks, far_count, nz
+    )
     return (current.reshape(expression.shape), covariance)
 
 

time: 256 us -> 246 us (0.961)
  Pallas kernels: 245 us -> 240 us
    pallas_call x1, Pallas kernels: 245 us -> 240 us  [diffuse(): pl.pallas_call(functools.partial(diffuse_kernel, nz, 1.0 / (shards * BLK...]
where the time goes in v4:
time: 246 us; the launch traced here: 244 us
  Pallas kernels  240 us (98%)
  local copies, waits for them, and re-layouts  3.74 us (2%)
    pallas_call x1, Pallas kernels, diffuse(): pl.pallas_call(functools.partial(diffuse_kernel, nz, 1.0 / (shards * BLK...  240 us

profile of v4, /device:TPU:33, one launch (start us, length us, event | category | flops | bytes accessed | tf_op | source)
XLA Modules:
  0.0 244.2 jit_solution(13679977493203825726)
XLA Ops:
  0.6 239.8 %shard_map.68 = (bf16[8,128,512]{2,1,0:T(8,128)(2,1)}, f32[32,512]{1,0:T(8,128)}) custom-call(bf16[8,128,512]{2,1,0:T(8,128)(2,1)} %bitcast.3, bf16[8,12,128,128]{3,2,1,0:T(8,128)(2,1)} %aff.1, s32[4,8]{1,0:T(4,128)} %bitcast.5, s32[8,8]{1,0:T(8,128)} %far.1, s32[8]{0:T(128)} %count.1), custom_call_target="tpu_custom_call" | custom-call | tf_op jit(solution)/shard_map/pallas_call | solution.py:394
  240.4 2.3 copy.9
  242.7 1.5 copy.10

commit v5 on v4

--- a/solution.py
+++ b/solution.py
@@ -114,7 +114,7 @@
         ref = wsub(wrap(x + (3, 1, 2)[e], NX), half, i)
         return remote(ref, ref, wy_s.at[e, i], wy_r.at[e, i], up if i < 2 else down)
 
-    for n in range(2):
+    for n in range(4):
         w_first(0, n).start()
         w_first(1, n).start()
     own_w.start()
@@ -127,8 +127,6 @@
                 if n < 2:
                     w_forward(way, n).start()
                 w_across(way, i).start()
-                if n < 2:
-                    w_first(way, n + 2).start()
             else:
                 w_forward(way, n - 4).wait_recv()
                 w_across(2, i).start()
@@ -182,12 +180,13 @@
 
             p_copy(n, buf, 4 + flow_len + r, other).start()
 
-    def partner_done(n, buf):
+    def partner_own(n, buf):
         @pl.loop(0, 4)
         def _(j):
             p_copy(n, buf, j, shard_of(z, j, 1 - core)).wait_recv()
 
-        @pl.loop(0, flow_len)
+    def partner_done(n, buf, first, last):
+        @pl.loop(first, last)
         def _(r):
             p_copy(n, buf, 4 + r, from_left(r, 1 - core)).wait_recv()
             p_copy(n, buf, 4 + flow_len + r, from_right(r, 1 - core)).wait_recv()
@@ -228,22 +227,23 @@
     for j in (1, 3, 2):
         deal(j).wait_recv()
         send_own(0, x0, j)
-    cuts = (0, 3, 4, 6, 7, 8, 9, flow_len)
-    for part in range(7):
+    cuts = (0, 4, 6, 8, 9, 11, 12)
+    for part in range(6):
         pass_on(0, x0, cuts[part], cuts[part + 1])
-        if part < 6:
-            w_serve(part)
-
+        w_serve(part)
     for d in (1, 2, 3):
         names(d).wait_recv()
     to_smem = pltpu.make_async_copy(lv, ls, loc.at[1])
     to_smem.start()
+    partner_own(0, x0)
+    partner_done(0, x0, 0, 9)
     to_smem.wait()
     own_w.wait()
-    partner_done(0, x0)
+    pass_on(0, x0, 12, flow_len)
     for e in range(3):
         for i in range(4):
             w_across(e, i).wait_recv()
+    partner_done(0, x0, 9, flow_len)
 
     @pl.loop(0, NX)
     def _(j):
@@ -256,8 +256,23 @@
 
         send_own(1, x1, j)
 
-    pass_on(1, x1, 0, flow_len)
-    partner_done(1, x1)
+    pass_on(1, x1, 0, 8)
+    for d in (1, 2, 3):
+        deal(d).wait_send()
+        names(d).wait_send()
+        for i in range(4):
+            w_across(d - 1, i).wait_send()
+    for way in range(2):
+        for n in range(2):
+            w_forward(way, n).wait_send()
+        for n in range(4):
+            w_first(way, n).wait_send()
+    sends_done(0, x0)
+    pass_on(1, x1, 8, 12)
+    partner_own(1, x1)
+    partner_done(1, x1, 0, 9)
+    pass_on(1, x1, 12, flow_len)
+    partner_done(1, x1, 9, flow_len)
 
     def turn_x(way, n, xt, xc):
         ref = sx.at[xt, xc]
@@ -318,6 +333,7 @@
 
     product([y, yd, yu], [x, xl])
     product([y, yd, yu], [xr])
+    sends_done(1, x1)
     for j in range(2):
         turn_x(0, 4 + j, xo, wrap(xo - j, NX)).wait_recv()
         turn_y(0, 4 + j, yo, wrap(x - j, NX)).wait_recv()
@@ -348,6 +364,14 @@
         def _():
             to_owner(n).start()
 
+    for way in range(2):
+        for n in range(6):
+            turn_x(way, n, x, x).wait_send()
+            turn_y(way, n, y, x).wait_send()
+    for xt in range(NX):
+        write_out(xt).wait()
+    other.wait_send()
+
     @pl.when(source(z) == me)
     def _():
         r3[z] = rz[z // 2, lax.rem(x, 2)]
@@ -361,29 +385,10 @@
     for zz in range(1, nz):
         total += r3[zz].astype(jnp.float32)
     cov[...] = total * scale
-
-    for d in (1, 2, 3):
-        deal(d).wait_send()
-        names(d).wait_send()
-        for i in range(4):
-            w_across(d - 1, i).wait_send()
-    for way in range(2):
-        for n in range(2):
-            w_forward(way, n).wait_send()
-        for n in range(4):
-            w_first(way, n).wait_send()
-        for n in range(6):
-            turn_x(way, n, x, x).wait_send()
-            turn_y(way, n, y, x).wait_send()
-    sends_done(0, x0)
-    sends_done(1, x1)
-    other.wait_send()
     for n in range(nz):
         @pl.when(sink(n) != me)
         def _():
             to_owner(n).wait_send()
-    for xt in range(NX):
-        write_out(xt).wait()
 
 
 def diffuse(expression, affinity, near, far, count, nz):

time: 246 us -> 243 us (0.988)
  no operation moved by 1% of the time
where the time goes in v5:
time: 243 us; the launch traced here: 242 us
  Pallas kernels  238 us (98%)
  local copies, waits for them, and re-layouts  3.74 us (2%)
    pallas_call x1, Pallas kernels, diffuse(): pl.pallas_call(functools.partial(diffuse_kernel, nz, 1.0 / (shards * BLK...  238 us

profile of v5, /device:TPU:33, one launch (start us, length us, event | category | flops | bytes accessed | tf_op | source)
XLA Modules:
  0.0 242.4 jit_solution(16570066599701020038)
XLA Ops:
  0.6 238.0 %shard_map.68 = (bf16[8,128,512]{2,1,0:T(8,128)(2,1)}, f32[32,512]{1,0:T(8,128)}) custom-call(bf16[8,128,512]{2,1,0:T(8,128)(2,1)} %bitcast.3, bf16[8,12,128,128]{3,2,1,0:T(8,128)(2,1)} %aff.1, s32[4,8]{1,0:T(4,128)} %bitcast.5, s32[8,8]{1,0:T(8,128)} %far.1, s32[8]{0:T(128)} %count.1), custom_call_target="tpu_custom_call" | custom-call | tf_op jit(solution)/shard_map/pallas_call | solution.py:399
  238.7 2.3 copy.9
  240.9 1.5 copy.10

commit v6 on v5

--- a/solution.py
+++ b/solution.py
@@ -14,6 +14,7 @@
 BLK = 8
 SLOTS = 12
 LOC = 4
+HALF = BLK // 2
 
 
 def remote(src, dst, send, recv, device):
@@ -23,7 +24,8 @@
 
 
 def diffuse_kernel(
-    nz, scale, expr, aff, near, far, count, out, cov, x0, x1, w, lv, ls, sx, st, gram, r1, rz, r3,
+    nz, scale, expr, aff, near, far, count, out, cov, x0, x1a, x1b, w, lv, ls,
+    lanes, sx, st, whole, gram, r1, rz, r3,
     loc, xs_s, xs_r, li_s, li_r, wx_s, wx_r, wf_s, wf_r, wy_s, wy_r,
     z_s, z_r, p_s, p_r, g_s, g_r, a_s, a_r, c_s, c_r,
 ):
@@ -66,8 +68,8 @@
             pl.semaphore_signal(barrier, inc=1, device_id=(source(zz), y), device_id_type=MESH)
     pl.semaphore_wait(barrier, len(peers) + nz - jnp.where(source(z) == me, 1, 0))
 
-    def piece(buf, shard):
-        return buf.at[pl.ds(shard * BLK, BLK)]
+    def piece(buf, shard, size=BLK):
+        return buf.at[pl.ds(shard * size, size)]
 
     def columns(ref, xx):
         return ref.at[:, :, pl.ds(pl.multiple_of(xx * BL, BL), BL)]
@@ -83,9 +85,13 @@
         deal(d).start()
 
     slot = lax.broadcasted_iota(jnp.int32, (1, BLK), 1)
+    lv[x] = jnp.zeros((6 * BLK, BL), jnp.int32)
     for b in range(BLK):
         lv[x, b:b + 1, 0:BLK] = jnp.where(slot < count[b], far[b:b + 1, :], nz * 2 * NX * BLK)
     lv[x, BLK:BLK + LOC, 0:BLK] = near[...]
+    block = lv[x, 0:2 * BLK, :]
+    lv[x, 2 * BLK:4 * BLK, :] = (block >> 3) * HALF + (block & (HALF - 1))
+    lv[x, 4 * BLK:6 * BLK, :] = (block >> 2) & 1
 
     def names(d):
         return remote(lv.at[x], lv.at[x], li_s.at[d - 1], li_r.at[d - 1], x_dev(d))
@@ -135,13 +141,14 @@
         return cell(wrap(zz, nz), wrap(x - j, NX), kk)
 
     def z_copy(n, buf, way, s, shard):
+        ref = piece(buf, shard, BLK if n == 0 else HALF)
         return remote(
-            piece(buf, shard), piece(buf, shard), z_s.at[n, way, s], z_r.at[n, way, s],
-            right if way == 0 else left,
+            ref, ref, z_s.at[n, way, s], z_r.at[n, way, s], right if way == 0 else left
         )
 
     def p_copy(n, buf, q, shard):
-        return remote(piece(buf, shard), piece(buf, shard), p_s.at[n, q], p_r.at[n, q], partner)
+        ref = piece(buf, shard, BLK if n == 0 else HALF)
+        return remote(ref, ref, p_s.at[n, q], p_r.at[n, q], partner)
 
     def from_left(r, kk):
         return shard_of(z - 1 - r // 4, lax.rem(r, 4), kk)
@@ -156,29 +163,32 @@
         z_copy(n, buf, 1, j, shard).start()
         p_copy(n, buf, j, shard).start()
 
+    def pass_step(n, buf, r):
+        shard = from_left(r, core)
+        z_copy(n, buf, 0, r, shard).wait_recv()
+
+        @pl.when(r + 4 < flow_len)
+        def _():
+            z_copy(n, buf, 0, r + 4, shard).start()
+
+        p_copy(n, buf, 4 + r, shard).start()
+        other = from_right(r, core)
+        z_copy(n, buf, 1, r, other).wait_recv()
+
+        @pl.when(r < flow_len - 6)
+        def _():
+            z_copy(n, buf, 1, r + 4, other).start()
+
+        @pl.when((r >= flow_len - 4) & (r < flow_len - 2))
+        def _():
+            z_copy(n, buf, 1, r + 2, other).start()
+
+        p_copy(n, buf, 4 + flow_len + r, other).start()
+
     def pass_on(n, buf, first, last):
         @pl.loop(first, last)
         def _(r):
-            shard = from_left(r, core)
-            z_copy(n, buf, 0, r, shard).wait_recv()
-
-            @pl.when(r + 4 < flow_len)
-            def _():
-                z_copy(n, buf, 0, r + 4, shard).start()
-
-            p_copy(n, buf, 4 + r, shard).start()
-            other = from_right(r, core)
-            z_copy(n, buf, 1, r, other).wait_recv()
-
-            @pl.when(r < flow_len - 6)
-            def _():
-                z_copy(n, buf, 1, r + 4, other).start()
-
-            @pl.when((r >= flow_len - 4) & (r < flow_len - 2))
-            def _():
-                z_copy(n, buf, 1, r + 2, other).start()
-
-            p_copy(n, buf, 4 + flow_len + r, other).start()
+            pass_step(n, buf, r)
 
     def partner_own(n, buf):
         @pl.loop(0, 4)
@@ -203,24 +213,54 @@
         def _(q):
             p_copy(n, buf, q, shard).wait_send()
 
-    def name(xs, b, slot):
-        return ls[xs, BLK + slot, b] if slot < LOC else ls[xs, b, slot - LOC]
-
-    def block_sum(buf, xs, b):
+    def name(xs, b, slot, part=0):
+        first = 2 * BLK * part
+        return ls[xs, first + BLK + slot, b] if slot < LOC else ls[xs, first + b, slot - LOC]
+
+    def weighted(xs, b, rows):
         total = None
         for pair in range(SLOTS // 2):
-            rows = [buf[name(xs, b, 2 * pair + i)] for i in range(2)]
             mats = [w[xs, b, 2 * pair + i] for i in range(2)]
             term = jnp.dot(
-                jnp.concatenate(mats, axis=1), jnp.concatenate(rows, axis=0),
+                jnp.concatenate(mats, axis=1),
+                jnp.concatenate([rows(2 * pair), rows(2 * pair + 1)], axis=0),
                 preferred_element_type=jnp.float32,
             )
             total = term if total is None else total + term
-        return total.astype(jnp.bfloat16)
+        return total
+
+    on_left = lax.broadcasted_iota(jnp.int32, (BL, BL), 1) < BL // 2
+
+    def swap(tile):
+        return pltpu.roll(tile, BL // 2, 1)
+
+    def step_one(xs, p, shard):
+        low, high = [weighted(xs, b, lambda slot: x0[name(xs, b, slot)]) for b in (p, p + HALF)]
+        x1a[shard * HALF + p] = jnp.where(on_left, low, swap(high)).astype(jnp.bfloat16)
+        x1b[shard * HALF + p] = jnp.where(on_left, swap(low), high).astype(jnp.bfloat16)
+
+    def step_two(h, xs, p):
+        buf = x1a if h == 0 else x1b
+
+        def one(b):
+            def rows(slot):
+                tile = buf[name(xs, b, slot, 1)].reshape(BLK, BL // BLK, BL)
+                return (tile * lanes[name(xs, b, slot, 2)][None]).reshape(BL, BL)
+
+            both = weighted(xs, b, rows)
+            return both + swap(both)
+
+        tile = jnp.where(on_left, one(p), one(p + HALF)).astype(jnp.bfloat16)
+        sx[h, x, xs, p] = tile
+        st[h, y, :, pl.ds(pl.multiple_of((xs * HALF + p) * BL, BL), BL)] = tile.T
 
     zeros = jnp.zeros((BL, BL), jnp.bfloat16)
     x0[nz * 2 * NX * BLK] = zeros
-    x1[nz * 2 * NX * BLK] = zeros
+    x1a[nz * 2 * NX * HALF] = zeros
+    x1b[nz * 2 * NX * HALF] = zeros
+    for i in range(2):
+        keep = on_left if i == 0 else jnp.logical_not(on_left)
+        lanes[i] = jnp.where(keep, 1.0, 0.0)[0:BL // BLK].astype(jnp.bfloat16)
 
     own_in.wait()
     send_own(0, x0, 0)
@@ -247,16 +287,13 @@
 
     @pl.loop(0, NX)
     def _(j):
-        xs = wrap(x - j, NX)
-        base = shard_of(z, j, core) * BLK
-
-        @pl.loop(0, BLK)
-        def _(b):
-            x1[base + b] = block_sum(x0, xs, b)
-
-        send_own(1, x1, j)
-
-    pass_on(1, x1, 0, 8)
+        @pl.loop(0, HALF)
+        def _(p):
+            step_one(wrap(x - j, NX), p, shard_of(z, j, core))
+
+        send_own(1, x1a, j)
+
+    pass_on(1, x1a, 0, 8)
     for d in (1, 2, 3):
         deal(d).wait_send()
         names(d).wait_send()
@@ -268,89 +305,129 @@
         for n in range(4):
             w_first(way, n).wait_send()
     sends_done(0, x0)
-    pass_on(1, x1, 8, 12)
-    partner_own(1, x1)
-    partner_done(1, x1, 0, 9)
-    pass_on(1, x1, 12, flow_len)
-    partner_done(1, x1, 9, flow_len)
-
-    def turn_x(way, n, xt, xc):
-        ref = sx.at[xt, xc]
-        return remote(ref, ref, g_s.at[0, way, n], g_r.at[0, way, n], x_dev(1 if way == 0 else 3))
-
-    def turn_y(way, n, yt, xc):
-        ref = st.at[yt, xc]
-        return remote(ref, ref, g_s.at[1, way, n], g_r.at[1, way, n], up if way == 0 else down)
+    pass_on(1, x1a, 8, 10)
+
+    @pl.loop(10, flow_len)
+    def _(r):
+        pass_step(1, x1a, r)
+        send_own(2, x1b, r - 10)
+
+    partner_own(1, x1a)
+    partner_done(1, x1a, 0, flow_len)
+
+    def turn_x(h, way, n, xt, xc):
+        ref = sx.at[h, xt, xc]
+        return remote(
+            ref, ref, g_s.at[h, 0, way, n], g_r.at[h, 0, way, n], x_dev(1 if way == 0 else 3)
+        )
+
+    def turn_y(h, way, n, yt, xc):
+        ref = st.at[h, yt, :, pl.ds(pl.multiple_of(xc * HALF * BL, BL), HALF * BL)]
+        return remote(
+            ref, ref, g_s.at[h, 1, way, n], g_r.at[h, 1, way, n], up if way == 0 else down
+        )
+
+    xl, xr, xo = wrap(x - 1, NX), wrap(x + 1, NX), wrap(x + 2, NX)
+    yd, yu, yo = wrap(y - 1, NY), wrap(y + 1, NY), wrap(y + 2, NY)
+
+    def turn_own(h, j):
+        xc = wrap(x - j, NX)
+        for way in range(2):
+            turn_x(h, way, j, x, xc).start()
+            turn_y(h, way, j, y, xc).start()
+
+    def turn_step(h, j):
+        turn_x(h, 0, j, xl, wrap(xl - j, NX)).wait_recv()
+        turn_y(h, 0, j, yd, wrap(x - j, NX)).wait_recv()
+        if j < 2:
+            turn_x(h, 0, 4 + j, xl, wrap(xl - j, NX)).start()
+            turn_y(h, 0, 4 + j, yd, wrap(x - j, NX)).start()
+        turn_x(h, 1, j, xr, wrap(xr - j, NX)).wait_recv()
+        turn_y(h, 1, j, yu, wrap(x - j, NX)).wait_recv()
+        if j >= 2:
+            turn_x(h, 1, 2 + j, xr, wrap(xr - j, NX)).start()
+            turn_y(h, 1, 2 + j, yu, wrap(x - j, NX)).start()
+
+    def turn_end(h):
+        for j in range(2):
+            turn_x(h, 0, 4 + j, xo, wrap(xo - j, NX)).wait_recv()
+            turn_y(h, 0, 4 + j, yo, wrap(x - j, NX)).wait_recv()
+            turn_x(h, 1, 4 + j, xo, wrap(xo - 2 - j, NX)).wait_recv()
+            turn_y(h, 1, 4 + j, yo, wrap(x - 2 - j, NX)).wait_recv()
+
+    def product(hr, yts, hc, xts):
+        lhs = jnp.concatenate([st[hr, yt] for yt in yts], axis=0)
+        rhs = jnp.concatenate(
+            [sx[hc, xt].reshape(NX * HALF * BL, BL) for xt in xts], axis=1
+        )
+        part = jnp.dot(lhs, rhs, preferred_element_type=jnp.float32)
+        mid = BL // 2
+        for i, yt in enumerate(yts):
+            for k, xt in enumerate(xts):
+                cols = pl.ds(xt * BL if isinstance(xt, int) else pl.multiple_of(xt * BL, BL), BL)
+                upper = part[i * BL:i * BL + mid, k * BL:(k + 1) * BL]
+                lower = part[i * BL + mid:(i + 1) * BL, k * BL:(k + 1) * BL]
+                if hc == 0:
+                    tile = (upper + swap(lower)).reshape(2, 32, BL)
+                else:
+                    tile = (swap(upper) + lower).reshape(2, 32, BL)
+                    tile = jnp.where(on_left[0:mid].reshape(2, 32, BL), gram[yt, hr, :, :, cols], tile)
+                gram[yt, hr, :, :, cols] = tile
+
+    @pl.loop(0, 8)
+    def _(r):
+        pass_step(2, x1b, r)
+        j = r // 2
+        for i in range(2):
+            step_two(0, wrap(x - j, NX), 2 * lax.rem(r, 2) + i)
+
+        @pl.when(lax.rem(r, 2) == 1)
+        def _():
+            turn_own(0, j)
+
+    pass_on(2, x1b, 8, 11)
+    turn_step(0, 0)
+    turn_step(0, 1)
+    sends_done(1, x1a)
+    pass_on(2, x1b, 11, 13)
+    turn_step(0, 2)
+    turn_step(0, 3)
+    partner_own(2, x1b)
+    partner_done(2, x1b, 0, 10)
+    pass_on(2, x1b, 13, flow_len)
+    partner_done(2, x1b, 10, flow_len)
 
     @pl.loop(0, NX)
     def _(j):
-        xc = wrap(x - j, NX)
-
-        @pl.loop(0, BLK)
-        def _(b):
-            value = block_sum(x1, xc, b)
-            sx[x, xc, b] = value
-            st[y, xc, :, pl.ds(pl.multiple_of(b * BL, BL), BL)] = value.T
-
-        for way in range(2):
-            turn_x(way, j, x, xc).start()
-            turn_y(way, j, y, xc).start()
-
-    xl, xr, xo = wrap(x - 1, NX), wrap(x + 1, NX), wrap(x + 2, NX)
-    yd, yu, yo = wrap(y - 1, NY), wrap(y + 1, NY), wrap(y + 2, NY)
+        @pl.loop(0, HALF)
+        def _(p):
+            step_two(1, wrap(x - j, NX), p)
+
+        turn_own(1, j)
+
+    turn_end(0)
+    every = list(range(NY))
+    product(0, every, 0, [0, 1])
+    product(0, every, 0, [2, 3])
     for j in range(NX):
-        turn_x(0, j, xl, wrap(xl - j, NX)).wait_recv()
-        turn_y(0, j, yd, wrap(x - j, NX)).wait_recv()
-        if j < 2:
-            turn_x(0, 4 + j, xl, wrap(xl - j, NX)).start()
-            turn_y(0, 4 + j, yd, wrap(x - j, NX)).start()
-        turn_x(1, j, xr, wrap(xr - j, NX)).wait_recv()
-        turn_y(1, j, yu, wrap(x - j, NX)).wait_recv()
-        if j >= 2:
-            turn_x(1, 2 + j, xr, wrap(xr - j, NX)).start()
-            turn_y(1, 2 + j, yu, wrap(x - j, NX)).start()
-
-    def product(yts, xts):
-        @pl.loop(0, NX)
-        def _(xc):
-            lhs = jnp.concatenate([st[yt, xc] for yt in yts], axis=0)
-            rhs = jnp.concatenate(
-                [sx[xt, xc].reshape(BLK * BL, BL) for xt in xts], axis=1
-            )
-            part = jnp.dot(lhs, rhs, preferred_element_type=jnp.float32)
-            for i, yt in enumerate(yts):
-                for k, xt in enumerate(xts):
-                    cols = pl.ds(pl.multiple_of(xt * BL, BL), BL)
-                    tile = part[i * BL:(i + 1) * BL, k * BL:(k + 1) * BL].reshape(2, 2, 32, BL)
-
-                    @pl.when(xc == 0)
-                    def _():
-                        gram[yt, :, :, :, cols] = tile
-
-                    @pl.when(xc > 0)
-                    def _():
-                        gram[yt, :, :, :, cols] += tile
-
-    product([y, yd, yu], [x, xl])
-    product([y, yd, yu], [xr])
-    sends_done(1, x1)
-    for j in range(2):
-        turn_x(0, 4 + j, xo, wrap(xo - j, NX)).wait_recv()
-        turn_y(0, 4 + j, yo, wrap(x - j, NX)).wait_recv()
-        turn_x(1, 4 + j, xo, wrap(xo - 2 - j, NX)).wait_recv()
-        turn_y(1, 4 + j, yo, wrap(x - 2 - j, NX)).wait_recv()
-    product([y, yd, yu], [xo])
-    product([yo], [x, xl])
-    product([yo], [xr, xo])
+        turn_step(1, j)
+    near_y = [y, yd, yu]
+    product(1, near_y, 0, [0, 1])
+    product(1, near_y, 0, [2, 3])
+    product(0, every, 1, [x, xl])
+    product(0, every, 1, [xr])
+    product(1, near_y, 1, [x, xl])
+    product(1, near_y, 1, [xr])
+    turn_end(1)
+    product(0, every, 1, [xo])
+    product(1, near_y, 1, [xo])
+    product(1, [yo], 0, [0, 1])
+    product(1, [yo], 0, [2, 3])
+    product(1, [yo], 1, [x, xl])
+    product(1, [yo], 1, [xr, xo])
 
     other = remote(gram.at[:, :, 1 - core], r1, a_s.at[0], a_r.at[0], partner)
     other.start()
-
-    def write_out(xt):
-        return pltpu.make_async_copy(sx.at[xt, x], columns(out, xt), loc.at[xt])
-
-    for xt in range(NX):
-        write_out(xt).start()
 
     def to_owner(n):
         return remote(rz.at[n // 2, n % 2], r3.at[z], c_s.at[n], c_r.at[z], (sink(n), y))
@@ -364,12 +441,21 @@
         def _():
             to_owner(n).start()
 
-    for way in range(2):
-        for n in range(6):
-            turn_x(way, n, x, x).wait_send()
-            turn_y(way, n, y, x).wait_send()
     for xt in range(NX):
-        write_out(xt).wait()
+        cols = pl.ds(xt * BL, BL)
+        for p in range(HALF):
+            half_a = sx[0, xt, x, p].astype(jnp.float32)
+            half_b = sx[1, xt, x, p].astype(jnp.float32)
+            whole[p, :, cols] = jnp.where(on_left, half_a, swap(half_b)).astype(jnp.bfloat16)
+            whole[p + HALF, :, cols] = jnp.where(on_left, swap(half_a), half_b).astype(jnp.bfloat16)
+    own_out = pltpu.make_async_copy(whole, out, loc.at[0])
+    own_out.start()
+    for h in range(2):
+        for way in range(2):
+            for n in range(6):
+                turn_x(h, way, n, x, x).wait_send()
+                turn_y(h, way, n, y, x).wait_send()
+    sends_done(2, x1b)
     other.wait_send()
 
     @pl.when(source(z) == me)
@@ -389,6 +475,7 @@
         @pl.when(sink(n) != me)
         def _():
             to_owner(n).wait_send()
+    own_out.wait()
 
 
 def diffuse(expression, affinity, near, far, count, nz):
@@ -412,12 +499,15 @@
         out_specs=(any_spec, pl.BlockSpec(memory_space=pltpu.VMEM)),
         scratch_shapes=[
             pltpu.VMEM((shards * BLK + 1, BL, BL), jnp.bfloat16),
-            pltpu.VMEM((shards * BLK + 1, BL, BL), jnp.bfloat16),
+            pltpu.VMEM((shards * HALF + 1, BL, BL), jnp.bfloat16),
+            pltpu.VMEM((shards * HALF + 1, BL, BL), jnp.bfloat16),
             pltpu.VMEM((NX, BLK, SLOTS, BL, BL), jnp.bfloat16),
-            pltpu.VMEM((NX, 2 * BLK, BL), jnp.int32),
-            pltpu.SMEM((NX, 2 * BLK, BL), jnp.int32),
-            pltpu.VMEM((NX, NX, BLK, BL, BL), jnp.bfloat16),
-            pltpu.VMEM((NY, NX, BL, BLK * BL), jnp.bfloat16),
+            pltpu.VMEM((NX, 6 * BLK, BL), jnp.int32),
+            pltpu.SMEM((NX, 6 * BLK, BL), jnp.int32),
+            pltpu.VMEM((2, BL // BLK, BL), jnp.bfloat16),
+            pltpu.VMEM((2, NX, NX, HALF, BL, BL), jnp.bfloat16),
+            pltpu.VMEM((2, NY, BL, NX * HALF * BL), jnp.bfloat16),
+            pltpu.VMEM((BLK, BL, NX * BL), jnp.bfloat16),
             pltpu.VMEM((NY, 2, 2, 32, NX * BL), jnp.float32),
             pltpu.VMEM((NY, 2, 32, NX * BL), jnp.float32),
             pltpu.VMEM((NY, 2, 32, NX * BL), jnp.bfloat16),
@@ -428,9 +518,9 @@
             dma((2, 4)), dma((2, 4)),
             dma((2, 2)), dma((2, 2)),
             dma((3, 4)), dma((3, 4)),
-            dma((2, 2, flow_len)), dma((2, 2, flow_len)),
-            dma((2, 4 + 2 * flow_len)), dma((2, 4 + 2 * flow_len)),
-            dma((2, 2, 6)), dma((2, 2, 6)),
+            dma((3, 2, flow_len)), dma((3, 2, flow_len)),
+            dma((3, 4 + 2 * flow_len)), dma((3, 4 + 2 * flow_len)),
+            dma((2, 2, 2, 6)), dma((2, 2, 2, 6)),
             dma((1,)), dma((1,)),
             dma((nz,)), dma((nz,)),
         ],

time: 243 us -> 224 us (0.922)
  Pallas kernels: 238 us -> 219 us
    pallas_call x1, Pallas kernels: 238 us -> 219 us  [diffuse(): pl.pallas_call(functools.partial(diffuse_kernel, nz, 1.0 / (shards * BLK...]
where the time goes in v6:
time: 224 us
  Pallas kernels  219 us (98%)
  local copies, waits for them, and re-layouts  3.74 us (2%)
    pallas_call x1, Pallas kernels, diffuse(): pl.pallas_call(functools.partial(diffuse_kernel, nz, 1.0 / (shards * BLK...  219 us

profile of v6, /device:TPU:33, one launch (start us, length us, event | category | flops | bytes accessed | tf_op | source)
XLA Modules:
  0.0 223.5 jit_solution(4358276032008116192)
XLA Ops:
  0.6 219.2 %shard_map.68 = (bf16[8,128,512]{2,1,0:T(8,128)(2,1)}, f32[32,512]{1,0:T(8,128)}) custom-call(bf16[8,128,512]{2,1,0:T(8,128)(2,1)} %bitcast.3, bf16[8,12,128,128]{3,2,1,0:T(8,128)(2,1)} %aff.1, s32[4,8]{1,0:T(4,128)} %bitcast.5, s32[8,8]{1,0:T(8,128)} %far.1, s32[8]{0:T(128)} %count.1), custom_call_target="tpu_custom_call" | custom-call | tf_op jit(solution)/shard_map/pallas_call | solution.py:486
  219.8 2.3 %copy.9 = bf16[1024,512]{1,0:T(8,128)(2,1)} copy(bf16[1024,512]{1,0:T(8,128)(2,1)} %bitcast.4) | data formatting | bytes 2097152
  222.1 1.5 copy.10

commit v7 on v6

--- a/solution.py
+++ b/solution.py
@@ -25,8 +25,8 @@
 
 def diffuse_kernel(
     nz, scale, expr, aff, near, far, count, out, cov, x0, x1a, x1b, w, lv, ls,
-    lanes, sx, st, whole, gram, r1, rz, r3,
-    loc, xs_s, xs_r, li_s, li_r, wx_s, wx_r, wf_s, wf_r, wy_s, wy_r,
+    near_v, far_v, count_s, lanes, sx, st, whole, gram, r1, rz, r3,
+    loc, xs_s, xs_r, li_s, li_r, w_s, wx_r, wf_r, wy_r,
     z_s, z_r, p_s, p_r, g_s, g_r, a_s, a_r, c_s, c_r,
 ):
     flow_len = 4 * (nz // 2) - 2
@@ -66,7 +66,6 @@
         @pl.when(source(zz) != me)
         def _():
             pl.semaphore_signal(barrier, inc=1, device_id=(source(zz), y), device_id_type=MESH)
-    pl.semaphore_wait(barrier, len(peers) + nz - jnp.where(source(z) == me, 1, 0))
 
     def piece(buf, shard, size=BLK):
         return buf.at[pl.ds(shard * size, size)]
@@ -76,28 +75,12 @@
 
     def deal(d):
         return remote(
-            columns(expr, wrap(x + d, NX)), piece(x0, me), xs_s.at[d - 1], xs_r.at[d - 1], x_dev(d)
+            columns(expr, wrap(x + d, NX)), piece(x0, me), xs_s.at[0], xs_r.at[d - 1], x_dev(d)
         )
 
     own_in = pltpu.make_async_copy(columns(expr, x), piece(x0, me), loc.at[0])
-    own_in.start()
-    for d in (1, 3, 2):
-        deal(d).start()
-
-    slot = lax.broadcasted_iota(jnp.int32, (1, BLK), 1)
-    lv[x] = jnp.zeros((6 * BLK, BL), jnp.int32)
-    for b in range(BLK):
-        lv[x, b:b + 1, 0:BLK] = jnp.where(slot < count[b], far[b:b + 1, :], nz * 2 * NX * BLK)
-    lv[x, BLK:BLK + LOC, 0:BLK] = near[...]
-    block = lv[x, 0:2 * BLK, :]
-    lv[x, 2 * BLK:4 * BLK, :] = (block >> 3) * HALF + (block & (HALF - 1))
-    lv[x, 4 * BLK:6 * BLK, :] = (block >> 2) & 1
-
     def names(d):
-        return remote(lv.at[x], lv.at[x], li_s.at[d - 1], li_r.at[d - 1], x_dev(d))
-
-    for d in (1, 2, 3):
-        names(d).start()
+        return remote(lv.at[x], lv.at[x], li_s.at[0], li_r.at[0], x_dev(d))
 
     own_w = pltpu.make_async_copy(aff, w.at[x], loc.at[2])
 
@@ -107,23 +90,18 @@
     def w_first(way, n):
         i = n if way == 0 else 3 - n
         return remote(
-            aff.at[4 * half + i], wsub(x, half, i), wx_s.at[way, n], wx_r.at[way, n],
+            aff.at[4 * half + i], wsub(x, half, i), w_s.at[0], wx_r.at[way, n],
             x_dev(1 if way == 0 else 3),
         )
 
     def w_forward(way, n):
         i = n if way == 0 else 3 - n
         ref = wsub(wrap(x - 1, NX) if way == 0 else wrap(x + 1, NX), half, i)
-        return remote(ref, ref, wf_s.at[way, n], wf_r.at[way, n], x_dev(1 if way == 0 else 3))
+        return remote(ref, ref, w_s.at[0], wf_r.at[way, n], x_dev(1 if way == 0 else 3))
 
     def w_across(e, i):
         ref = wsub(wrap(x + (3, 1, 2)[e], NX), half, i)
-        return remote(ref, ref, wy_s.at[e, i], wy_r.at[e, i], up if i < 2 else down)
-
-    for n in range(4):
-        w_first(0, n).start()
-        w_first(1, n).start()
-    own_w.start()
+        return remote(ref, ref, w_s.at[0], wy_r.at[0], up if i < 2 else down)
 
     def w_serve(n):
         for way in range(2):
@@ -143,12 +121,12 @@
     def z_copy(n, buf, way, s, shard):
         ref = piece(buf, shard, BLK if n == 0 else HALF)
         return remote(
-            ref, ref, z_s.at[n, way, s], z_r.at[n, way, s], right if way == 0 else left
+            ref, ref, z_s.at[n], z_r.at[n % 2, way, s], right if way == 0 else left
         )
 
     def p_copy(n, buf, q, shard):
         ref = piece(buf, shard, BLK if n == 0 else HALF)
-        return remote(ref, ref, p_s.at[n, q], p_r.at[n, q], partner)
+        return remote(ref, ref, p_s.at[n], p_r.at[n], partner)
 
     def from_left(r, kk):
         return shard_of(z - 1 - r // 4, lax.rem(r, 4), kk)
@@ -190,28 +168,17 @@
         def _(r):
             pass_step(n, buf, r)
 
-    def partner_own(n, buf):
-        @pl.loop(0, 4)
-        def _(j):
-            p_copy(n, buf, j, shard_of(z, j, 1 - core)).wait_recv()
-
-    def partner_done(n, buf, first, last):
-        @pl.loop(first, last)
-        def _(r):
-            p_copy(n, buf, 4 + r, from_left(r, 1 - core)).wait_recv()
-            p_copy(n, buf, 4 + flow_len + r, from_right(r, 1 - core)).wait_recv()
+    def several(ref, send, recv):
+        return remote(ref, ref, send, recv, partner)
+
+    def partner_done(n, buf):
+        size = (BLK if n == 0 else HALF) * (4 + 2 * flow_len)
+        several(buf.at[pl.ds(0, size)], p_s.at[n], p_r.at[n]).wait_recv()
 
     def sends_done(n, buf):
-        shard = shard_of(z, 0, core)
-
-        @pl.loop(0, flow_len)
-        def _(s):
-            z_copy(n, buf, 0, s, shard).wait_send()
-            z_copy(n, buf, 1, s, shard).wait_send()
-
-        @pl.loop(0, 4 + 2 * flow_len)
-        def _(q):
-            p_copy(n, buf, q, shard).wait_send()
+        size = BLK if n == 0 else HALF
+        several(buf.at[pl.ds(0, size * 2 * flow_len)], z_s.at[n], p_r.at[n]).wait_send()
+        several(buf.at[pl.ds(0, size * (4 + 2 * flow_len))], p_s.at[n], p_r.at[n]).wait_send()
 
     def name(xs, b, slot, part=0):
         first = 2 * BLK * part
@@ -254,6 +221,15 @@
         sx[h, x, xs, p] = tile
         st[h, y, :, pl.ds(pl.multiple_of((xs * HALF + p) * BL, BL), BL)] = tile.T
 
+    small = [
+        pltpu.make_async_copy(near, near_v, loc.at[1]),
+        pltpu.make_async_copy(far, far_v, loc.at[3]),
+        pltpu.make_async_copy(count, count_s, loc.at[4]),
+    ]
+    for copy in small:
+        copy.start()
+    own_in.start()
+    own_w.start()
     zeros = jnp.zeros((BL, BL), jnp.bfloat16)
     x0[nz * 2 * NX * BLK] = zeros
     x1a[nz * 2 * NX * HALF] = zeros
@@ -261,9 +237,27 @@
     for i in range(2):
         keep = on_left if i == 0 else jnp.logical_not(on_left)
         lanes[i] = jnp.where(keep, 1.0, 0.0)[0:BL // BLK].astype(jnp.bfloat16)
-
+    for copy in small:
+        copy.wait()
+    slot = lax.broadcasted_iota(jnp.int32, (1, BLK), 1)
+    lv[x] = jnp.zeros((6 * BLK, BL), jnp.int32)
+    for b in range(BLK):
+        lv[x, b:b + 1, 0:BLK] = jnp.where(slot < count_s[b], far_v[b:b + 1, :], nz * 2 * NX * BLK)
+    lv[x, BLK:BLK + LOC, 0:BLK] = near_v[...]
+    block = lv[x, 0:2 * BLK, :]
+    lv[x, 2 * BLK:4 * BLK, :] = (block >> 3) * HALF + (block & (HALF - 1))
+    lv[x, 4 * BLK:6 * BLK, :] = (block >> 2) & 1
     own_in.wait()
+    pl.semaphore_wait(barrier, len(peers) + nz - jnp.where(source(z) == me, 1, 0))
+
     send_own(0, x0, 0)
+    for d in (1, 3, 2):
+        deal(d).start()
+    for d in (1, 2, 3):
+        names(d).start()
+    for n in range(4):
+        w_first(0, n).start()
+        w_first(1, n).start()
     for j in (1, 3, 2):
         deal(j).wait_recv()
         send_own(0, x0, j)
@@ -271,19 +265,14 @@
     for part in range(6):
         pass_on(0, x0, cuts[part], cuts[part + 1])
         w_serve(part)
-    for d in (1, 2, 3):
-        names(d).wait_recv()
+    several(lv.at[pl.ds(0, NX - 1)], li_s.at[0], li_r.at[0]).wait_recv()
     to_smem = pltpu.make_async_copy(lv, ls, loc.at[1])
     to_smem.start()
-    partner_own(0, x0)
-    partner_done(0, x0, 0, 9)
     to_smem.wait()
     own_w.wait()
     pass_on(0, x0, 12, flow_len)
-    for e in range(3):
-        for i in range(4):
-            w_across(e, i).wait_recv()
-    partner_done(0, x0, 9, flow_len)
+    several(w.at[pl.ds(0, 3), pl.ds(0, 4)], w_s.at[0], wy_r.at[0]).wait_recv()
+    partner_done(0, x0)
 
     @pl.loop(0, NX)
     def _(j):
@@ -294,16 +283,9 @@
         send_own(1, x1a, j)
 
     pass_on(1, x1a, 0, 8)
-    for d in (1, 2, 3):
-        deal(d).wait_send()
-        names(d).wait_send()
-        for i in range(4):
-            w_across(d - 1, i).wait_send()
-    for way in range(2):
-        for n in range(2):
-            w_forward(way, n).wait_send()
-        for n in range(4):
-            w_first(way, n).wait_send()
+    several(piece(x0, 0, 3 * BLK), xs_s.at[0], xs_r.at[0]).wait_send()
+    several(lv.at[pl.ds(0, NX - 1)], li_s.at[0], li_r.at[0]).wait_send()
+    several(w.at[pl.ds(0, 3)], w_s.at[0], wy_r.at[0]).wait_send()
     sends_done(0, x0)
     pass_on(1, x1a, 8, 10)
 
@@ -312,19 +294,21 @@
         pass_step(1, x1a, r)
         send_own(2, x1b, r - 10)
 
-    partner_own(1, x1a)
-    partner_done(1, x1a, 0, flow_len)
+    partner_done(1, x1a)
+
+    def passed(n):
+        return min(n, 4) if isinstance(n, int) else n
 
     def turn_x(h, way, n, xt, xc):
         ref = sx.at[h, xt, xc]
         return remote(
-            ref, ref, g_s.at[h, 0, way, n], g_r.at[h, 0, way, n], x_dev(1 if way == 0 else 3)
+            ref, ref, g_s.at[h, 0], g_r.at[h, 0, way, passed(n)], x_dev(1 if way == 0 else 3)
         )
 
     def turn_y(h, way, n, yt, xc):
         ref = st.at[h, yt, :, pl.ds(pl.multiple_of(xc * HALF * BL, BL), HALF * BL)]
         return remote(
-            ref, ref, g_s.at[h, 1, way, n], g_r.at[h, 1, way, n], up if way == 0 else down
+            ref, ref, g_s.at[h, 1], g_r.at[h, 1, way, passed(n)], up if way == 0 else down
         )
 
     xl, xr, xo = wrap(x - 1, NX), wrap(x + 1, NX), wrap(x + 2, NX)
@@ -349,11 +333,9 @@
             turn_y(h, 1, 2 + j, yu, wrap(x - j, NX)).start()
 
     def turn_end(h):
-        for j in range(2):
-            turn_x(h, 0, 4 + j, xo, wrap(xo - j, NX)).wait_recv()
-            turn_y(h, 0, 4 + j, yo, wrap(x - j, NX)).wait_recv()
-            turn_x(h, 1, 4 + j, xo, wrap(xo - 2 - j, NX)).wait_recv()
-            turn_y(h, 1, 4 + j, yo, wrap(x - 2 - j, NX)).wait_recv()
+        for way in range(2):
+            several(sx.at[h, 0, pl.ds(0, 2)], g_s.at[h, 0], g_r.at[h, 0, way, 4]).wait_recv()
+            several(st.at[h, 0, :, pl.ds(0, 2 * HALF * BL)], g_s.at[h, 1], g_r.at[h, 1, way, 4]).wait_recv()
 
     def product(hr, yts, hc, xts):
         lhs = jnp.concatenate([st[hr, yt] for yt in yts], axis=0)
@@ -392,10 +374,8 @@
     pass_on(2, x1b, 11, 13)
     turn_step(0, 2)
     turn_step(0, 3)
-    partner_own(2, x1b)
-    partner_done(2, x1b, 0, 10)
     pass_on(2, x1b, 13, flow_len)
-    partner_done(2, x1b, 10, flow_len)
+    partner_done(2, x1b)
 
     @pl.loop(0, NX)
     def _(j):
@@ -430,7 +410,7 @@
     other.start()
 
     def to_owner(n):
-        return remote(rz.at[n // 2, n % 2], r3.at[z], c_s.at[n], c_r.at[z], (sink(n), y))
+        return remote(rz.at[n // 2, n % 2], r3.at[z], c_s.at[0], c_r.at[0], (sink(n), y))
 
     other.wait_recv()
     for n in range(nz):
@@ -451,10 +431,8 @@
     own_out = pltpu.make_async_copy(whole, out, loc.at[0])
     own_out.start()
     for h in range(2):
-        for way in range(2):
-            for n in range(6):
-                turn_x(h, way, n, x, x).wait_send()
-                turn_y(h, way, n, y, x).wait_send()
+        several(sx.at[h, pl.ds(0, 3)], g_s.at[h, 0], g_r.at[h, 0, 0, 4]).wait_send()
+        several(st.at[h, pl.ds(0, 3)], g_s.at[h, 1], g_r.at[h, 1, 0, 4]).wait_send()
     sends_done(2, x1b)
     other.wait_send()
 
@@ -462,19 +440,21 @@
     def _():
         r3[z] = rz[z // 2, lax.rem(x, 2)]
 
-    for zz in range(nz):
-        @pl.when(source(zz) != me)
-        def _():
-            remote(rz.at[0, 0], r3.at[zz], c_s.at[0], c_r.at[zz], (source(zz), y)).wait_recv()
-
+    def all_sums(do):
+        @pl.when(source(z) == me)
+        def _():
+            do(several(r3.at[pl.ds(0, nz - 1)], c_s.at[0], c_r.at[0]))
+
+        @pl.when(source(z) != me)
+        def _():
+            do(several(r3, c_s.at[0], c_r.at[0]))
+
+    all_sums(lambda copies: copies.wait_recv())
     total = r3[0].astype(jnp.float32)
     for zz in range(1, nz):
         total += r3[zz].astype(jnp.float32)
     cov[...] = total * scale
-    for n in range(nz):
-        @pl.when(sink(n) != me)
-        def _():
-            to_owner(n).wait_send()
+    all_sums(lambda copies: copies.wait_send())
     own_out.wait()
 
 
@@ -489,13 +469,7 @@
             jax.ShapeDtypeStruct(expression.shape, jnp.bfloat16),
             jax.ShapeDtypeStruct((32, NX * BL), jnp.float32),
         ),
-        in_specs=[
-            any_spec,
-            any_spec,
-            pl.BlockSpec(memory_space=pltpu.VMEM),
-            pl.BlockSpec(memory_space=pltpu.VMEM),
-            pl.BlockSpec(memory_space=pltpu.SMEM),
-        ],
+        in_specs=[any_spec] * 5,
         out_specs=(any_spec, pl.BlockSpec(memory_space=pltpu.VMEM)),
         scratch_shapes=[
             pltpu.VMEM((shards * BLK + 1, BL, BL), jnp.bfloat16),
@@ -504,6 +478,9 @@
             pltpu.VMEM((NX, BLK, SLOTS, BL, BL), jnp.bfloat16),
             pltpu.VMEM((NX, 6 * BLK, BL), jnp.int32),
             pltpu.SMEM((NX, 6 * BLK, BL), jnp.int32),
+            pltpu.VMEM((LOC, BLK), jnp.int32),
+            pltpu.VMEM((BLK, BLK), jnp.int32),
+            pltpu.SMEM((BLK,), jnp.int32),
             pltpu.VMEM((2, BL // BLK, BL), jnp.bfloat16),
             pltpu.VMEM((2, NX, NX, HALF, BL, BL), jnp.bfloat16),
             pltpu.VMEM((2, NY, BL, NX * HALF * BL), jnp.bfloat16),
@@ -512,17 +489,15 @@
             pltpu.VMEM((NY, 2, 32, NX * BL), jnp.float32),
             pltpu.VMEM((NY, 2, 32, NX * BL), jnp.bfloat16),
             pltpu.VMEM((nz, 32, NX * BL), jnp.bfloat16),
-            dma((4,)),
+            dma((5,)),
+            dma((1,)), dma((3,)),
+            dma((1,)), dma((1,)),
+            dma((1,)), dma((2, 4)), dma((2, 2)), dma((1,)),
+            dma((3,)), dma((2, 2, flow_len)),
             dma((3,)), dma((3,)),
-            dma((3,)), dma((3,)),
-            dma((2, 4)), dma((2, 4)),
-            dma((2, 2)), dma((2, 2)),
-            dma((3, 4)), dma((3, 4)),
-            dma((3, 2, flow_len)), dma((3, 2, flow_len)),
-            dma((3, 4 + 2 * flow_len)), dma((3, 4 + 2 * flow_len)),
-            dma((2, 2, 2, 6)), dma((2, 2, 2, 6)),
+            dma((2, 2)), dma((2, 2, 2, 5)),
             dma((1,)), dma((1,)),
-            dma((nz,)), dma((nz,)),
+            dma((1,)), dma((1,)),
         ],
         compiler_params=pltpu.CompilerParams(
             collective_id=0, has_side_effects=True, vmem_limit_bytes=60 * 2**20

time: 224 us -> 219 us (0.978)
  Pallas kernels: 219 us -> 215 us
    pallas_call x1, Pallas kernels: 219 us -> 215 us  [diffuse(): pl.pallas_call(functools.partial(diffuse_kernel, nz, 1.0 / (shards * BLK...]
where the time goes in v7:
time: 219 us
  Pallas kernels  215 us (98%)
  local copies, waits for them, and re-layouts  3.74 us (2%)
    pallas_call x1, Pallas kernels, diffuse(): pl.pallas_call(functools.partial(diffuse_kernel, nz, 1.0 / (shards * BLK...  215 us

profile of v7, /device:TPU:33, one launch (start us, length us, event | category | flops | bytes accessed | tf_op | source)
XLA Modules:
  0.0 219.2 jit_solution(9603146325835157549)
XLA Ops:
  0.6 214.8 %shard_map.68 = (bf16[8,128,512]{2,1,0:T(8,128)(2,1)}, f32[32,512]{1,0:T(8,128)}) custom-call(bf16[8,128,512]{2,1,0:T(8,128)(2,1)} %bitcast.3, bf16[8,12,128,128]{3,2,1,0:T(8,128)(2,1)} %aff.1, s32[4,8]{1,0:T(4,128)} %bitcast.5, s32[8,8]{1,0:T(8,128)} %far.1, s32[8]{0:T(128)} %count.1), custom_call_target="tpu_custom_call" | custom-call | tf_op jit(solution)/shard_map/pallas_call | solution.py:466
  215.4 2.3 %copy.9 = bf16[1024,512]{1,0:T(8,128)(2,1)} copy(bf16[1024,512]{1,0:T(8,128)(2,1)} %bitcast.4) | data formatting | bytes 2097152
  217.7 1.5 copy.10

commit v8 on v7

--- a/solution.py
+++ b/solution.py
@@ -29,7 +29,6 @@
     loc, xs_s, xs_r, li_s, li_r, w_s, wx_r, wf_r, wy_r,
     z_s, z_r, p_s, p_r, g_s, g_r, a_s, a_r, c_s, c_r,
 ):
-    flow_len = 4 * (nz // 2) - 2
     me = lax.axis_index("cells")
     y = lax.axis_index("genes")
     core = lax.rem(me, 2)
@@ -115,53 +114,69 @@
                 w_forward(way, n - 4).wait_recv()
                 w_across(2, i).start()
 
+    def unit(n):
+        return NX if n == 0 else 2 * NX
+
+    def flow_len(n):
+        return unit(n) * (nz // 2) - unit(n) // 2
+
     def shard_of(zz, j, kk):
         return cell(wrap(zz, nz), wrap(x - j, NX), kk)
 
-    def z_copy(n, buf, way, s, shard):
-        ref = piece(buf, shard, BLK if n == 0 else HALF)
+    def place(n, zz, q, kk):
+        if n == 0:
+            return shard_of(zz, q, kk) * BLK
+        return shard_of(zz, q // 2, kk) * HALF + 2 * lax.rem(q, 2)
+
+    def part_of(n, buf, first):
+        return buf.at[pl.ds(first, BLK if n == 0 else 2)]
+
+    def z_copy(n, buf, way, s, first):
+        ref = part_of(n, buf, first)
         return remote(
             ref, ref, z_s.at[n], z_r.at[n % 2, way, s], right if way == 0 else left
         )
 
-    def p_copy(n, buf, q, shard):
-        ref = piece(buf, shard, BLK if n == 0 else HALF)
+    def p_copy(n, buf, first):
+        ref = part_of(n, buf, first)
         return remote(ref, ref, p_s.at[n], p_r.at[n], partner)
 
-    def from_left(r, kk):
-        return shard_of(z - 1 - r // 4, lax.rem(r, 4), kk)
-
-    def from_right(r, kk):
-        j = lax.rem(r, 4) + jnp.where(r < flow_len - 2, 0, 2)
-        return shard_of(z + 1 + r // 4, j, kk)
-
-    def send_own(n, buf, j):
-        shard = shard_of(z, j, core)
-        z_copy(n, buf, 0, j, shard).start()
-        z_copy(n, buf, 1, j, shard).start()
-        p_copy(n, buf, j, shard).start()
+    def from_left(n, r, kk):
+        return place(n, z - 1 - r // unit(n), lax.rem(r, unit(n)), kk)
+
+    def from_right(n, r, kk):
+        half_unit = unit(n) // 2
+        q = lax.rem(r, unit(n)) + jnp.where(r < flow_len(n) - half_unit, 0, half_unit)
+        return place(n, z + 1 + r // unit(n), q, kk)
+
+    def send_own(n, buf, q):
+        first = place(n, z, q, core)
+        z_copy(n, buf, 0, q, first).start()
+        z_copy(n, buf, 1, q, first).start()
+        p_copy(n, buf, first).start()
 
     def pass_step(n, buf, r):
-        shard = from_left(r, core)
-        z_copy(n, buf, 0, r, shard).wait_recv()
-
-        @pl.when(r + 4 < flow_len)
-        def _():
-            z_copy(n, buf, 0, r + 4, shard).start()
-
-        p_copy(n, buf, 4 + r, shard).start()
-        other = from_right(r, core)
+        size, last = unit(n), flow_len(n)
+        first = from_left(n, r, core)
+        z_copy(n, buf, 0, r, first).wait_recv()
+
+        @pl.when(r + size < last)
+        def _():
+            z_copy(n, buf, 0, r + size, first).start()
+
+        p_copy(n, buf, first).start()
+        other = from_right(n, r, core)
         z_copy(n, buf, 1, r, other).wait_recv()
 
-        @pl.when(r < flow_len - 6)
-        def _():
-            z_copy(n, buf, 1, r + 4, other).start()
-
-        @pl.when((r >= flow_len - 4) & (r < flow_len - 2))
-        def _():
-            z_copy(n, buf, 1, r + 2, other).start()
-
-        p_copy(n, buf, 4 + flow_len + r, other).start()
+        @pl.when(r < last - size - size // 2)
+        def _():
+            z_copy(n, buf, 1, r + size, other).start()
+
+        @pl.when((r >= last - size) & (r < last - size // 2))
+        def _():
+            z_copy(n, buf, 1, r + size // 2, other).start()
+
+        p_copy(n, buf, other).start()
 
     def pass_on(n, buf, first, last):
         @pl.loop(first, last)
@@ -172,29 +187,25 @@
         return remote(ref, ref, send, recv, partner)
 
     def partner_done(n, buf):
-        size = (BLK if n == 0 else HALF) * (4 + 2 * flow_len)
+        size = (BLK if n == 0 else 2) * (unit(n) + 2 * flow_len(n))
         several(buf.at[pl.ds(0, size)], p_s.at[n], p_r.at[n]).wait_recv()
 
     def sends_done(n, buf):
-        size = BLK if n == 0 else HALF
-        several(buf.at[pl.ds(0, size * 2 * flow_len)], z_s.at[n], p_r.at[n]).wait_send()
-        several(buf.at[pl.ds(0, size * (4 + 2 * flow_len))], p_s.at[n], p_r.at[n]).wait_send()
+        size = BLK if n == 0 else 2
+        z_all, p_all = size * 2 * flow_len(n), size * (unit(n) + 2 * flow_len(n))
+        several(buf.at[pl.ds(0, z_all)], z_s.at[n], p_r.at[n]).wait_send()
+        several(buf.at[pl.ds(0, p_all)], p_s.at[n], p_r.at[n]).wait_send()
 
     def name(xs, b, slot, part=0):
         first = 2 * BLK * part
         return ls[xs, first + BLK + slot, b] if slot < LOC else ls[xs, first + b, slot - LOC]
 
     def weighted(xs, b, rows):
-        total = None
-        for pair in range(SLOTS // 2):
-            mats = [w[xs, b, 2 * pair + i] for i in range(2)]
-            term = jnp.dot(
-                jnp.concatenate(mats, axis=1),
-                jnp.concatenate([rows(2 * pair), rows(2 * pair + 1)], axis=0),
-                preferred_element_type=jnp.float32,
-            )
-            total = term if total is None else total + term
-        return total
+        return jnp.dot(
+            jnp.concatenate([w[xs, b, slot] for slot in range(SLOTS)], axis=1),
+            jnp.concatenate([rows(slot) for slot in range(SLOTS)], axis=0),
+            preferred_element_type=jnp.float32,
+        )
 
     on_left = lax.broadcasted_iota(jnp.int32, (BL, BL), 1) < BL // 2
 
@@ -270,43 +281,43 @@
     to_smem.start()
     to_smem.wait()
     own_w.wait()
-    pass_on(0, x0, 12, flow_len)
+    pass_on(0, x0, 12, flow_len(0))
     several(w.at[pl.ds(0, 3), pl.ds(0, 4)], w_s.at[0], wy_r.at[0]).wait_recv()
     partner_done(0, x0)
 
-    @pl.loop(0, NX)
-    def _(j):
-        @pl.loop(0, HALF)
-        def _(p):
-            step_one(wrap(x - j, NX), p, shard_of(z, j, core))
-
-        send_own(1, x1a, j)
-
-    pass_on(1, x1a, 0, 8)
+    @pl.loop(0, 2 * NX)
+    def _(q):
+        j = q // 2
+        for i in range(2):
+            step_one(wrap(x - j, NX), 2 * lax.rem(q, 2) + i, shard_of(z, j, core))
+        send_own(1, x1a, q)
+
+    pass_on(1, x1a, 0, 16)
     several(piece(x0, 0, 3 * BLK), xs_s.at[0], xs_r.at[0]).wait_send()
     several(lv.at[pl.ds(0, NX - 1)], li_s.at[0], li_r.at[0]).wait_send()
     several(w.at[pl.ds(0, 3)], w_s.at[0], wy_r.at[0]).wait_send()
     sends_done(0, x0)
-    pass_on(1, x1a, 8, 10)
-
-    @pl.loop(10, flow_len)
+    pass_on(1, x1a, 16, 20)
+
+    @pl.loop(20, flow_len(1))
     def _(r):
         pass_step(1, x1a, r)
-        send_own(2, x1b, r - 10)
+        send_own(2, x1b, r - 20)
 
     partner_done(1, x1a)
 
     def passed(n):
-        return min(n, 4) if isinstance(n, int) else n
-
-    def turn_x(h, way, n, xt, xc):
-        ref = sx.at[h, xt, xc]
+        return min(n, 8) if isinstance(n, int) else n
+
+    def turn_x(h, way, n, xt, q):
+        ref = sx.at[h, xt, wrap(xt - q // 2, NX), pl.ds(2 * (q % 2), 2)]
         return remote(
             ref, ref, g_s.at[h, 0], g_r.at[h, 0, way, passed(n)], x_dev(1 if way == 0 else 3)
         )
 
-    def turn_y(h, way, n, yt, xc):
-        ref = st.at[h, yt, :, pl.ds(pl.multiple_of(xc * HALF * BL, BL), HALF * BL)]
+    def turn_y(h, way, n, yt, q):
+        first = wrap(x - q // 2, NX) * 2 + q % 2
+        ref = st.at[h, yt, :, pl.ds(pl.multiple_of(first * 2 * BL, 2 * BL), 2 * BL)]
         return remote(
             ref, ref, g_s.at[h, 1], g_r.at[h, 1, way, passed(n)], up if way == 0 else down
         )
@@ -314,28 +325,27 @@
     xl, xr, xo = wrap(x - 1, NX), wrap(x + 1, NX), wrap(x + 2, NX)
     yd, yu, yo = wrap(y - 1, NY), wrap(y + 1, NY), wrap(y + 2, NY)
 
-    def turn_own(h, j):
-        xc = wrap(x - j, NX)
+    def turn_own(h, q):
         for way in range(2):
-            turn_x(h, way, j, x, xc).start()
-            turn_y(h, way, j, y, xc).start()
-
-    def turn_step(h, j):
-        turn_x(h, 0, j, xl, wrap(xl - j, NX)).wait_recv()
-        turn_y(h, 0, j, yd, wrap(x - j, NX)).wait_recv()
-        if j < 2:
-            turn_x(h, 0, 4 + j, xl, wrap(xl - j, NX)).start()
-            turn_y(h, 0, 4 + j, yd, wrap(x - j, NX)).start()
-        turn_x(h, 1, j, xr, wrap(xr - j, NX)).wait_recv()
-        turn_y(h, 1, j, yu, wrap(x - j, NX)).wait_recv()
-        if j >= 2:
-            turn_x(h, 1, 2 + j, xr, wrap(xr - j, NX)).start()
-            turn_y(h, 1, 2 + j, yu, wrap(x - j, NX)).start()
+            turn_x(h, way, q, x, q).start()
+            turn_y(h, way, q, y, q).start()
+
+    def turn_step(h, q):
+        turn_x(h, 0, q, xl, q).wait_recv()
+        turn_y(h, 0, q, yd, q).wait_recv()
+        if q < 4:
+            turn_x(h, 0, 8 + q, xl, q).start()
+            turn_y(h, 0, 8 + q, yd, q).start()
+        turn_x(h, 1, q, xr, q).wait_recv()
+        turn_y(h, 1, q, yu, q).wait_recv()
+        if q >= 4:
+            turn_x(h, 1, 4 + q, xr, q).start()
+            turn_y(h, 1, 4 + q, yu, q).start()
 
     def turn_end(h):
         for way in range(2):
-            several(sx.at[h, 0, pl.ds(0, 2)], g_s.at[h, 0], g_r.at[h, 0, way, 4]).wait_recv()
-            several(st.at[h, 0, :, pl.ds(0, 2 * HALF * BL)], g_s.at[h, 1], g_r.at[h, 1, way, 4]).wait_recv()
+            several(sx.at[h, 0, pl.ds(0, 2)], g_s.at[h, 0], g_r.at[h, 0, way, 8]).wait_recv()
+            several(st.at[h, 0, :, pl.ds(0, 2 * HALF * BL)], g_s.at[h, 1], g_r.at[h, 1, way, 8]).wait_recv()
 
     def product(hr, yts, hc, xts):
         lhs = jnp.concatenate([st[hr, yt] for yt in yts], axis=0)
@@ -356,41 +366,37 @@
                     tile = jnp.where(on_left[0:mid].reshape(2, 32, BL), gram[yt, hr, :, :, cols], tile)
                 gram[yt, hr, :, :, cols] = tile
 
-    @pl.loop(0, 8)
+    @pl.loop(0, 16)
     def _(r):
         pass_step(2, x1b, r)
-        j = r // 2
+        step_two(0, wrap(x - r // 4, NX), lax.rem(r, 4))
+
+        @pl.when(lax.rem(r, 2) == 1)
+        def _():
+            turn_own(0, r // 2)
+
+    pass_on(2, x1b, 16, 22)
+    for q in range(4):
+        turn_step(0, q)
+    sends_done(1, x1a)
+    pass_on(2, x1b, 22, 26)
+    for q in range(4, 8):
+        turn_step(0, q)
+    pass_on(2, x1b, 26, flow_len(2))
+    partner_done(2, x1b)
+
+    @pl.loop(0, 2 * NX)
+    def _(q):
         for i in range(2):
-            step_two(0, wrap(x - j, NX), 2 * lax.rem(r, 2) + i)
-
-        @pl.when(lax.rem(r, 2) == 1)
-        def _():
-            turn_own(0, j)
-
-    pass_on(2, x1b, 8, 11)
-    turn_step(0, 0)
-    turn_step(0, 1)
-    sends_done(1, x1a)
-    pass_on(2, x1b, 11, 13)
-    turn_step(0, 2)
-    turn_step(0, 3)
-    pass_on(2, x1b, 13, flow_len)
-    partner_done(2, x1b)
-
-    @pl.loop(0, NX)
-    def _(j):
-        @pl.loop(0, HALF)
-        def _(p):
-            step_two(1, wrap(x - j, NX), p)
-
-        turn_own(1, j)
+            step_two(1, wrap(x - q // 2, NX), 2 * lax.rem(q, 2) + i)
+        turn_own(1, q)
 
     turn_end(0)
     every = list(range(NY))
     product(0, every, 0, [0, 1])
     product(0, every, 0, [2, 3])
-    for j in range(NX):
-        turn_step(1, j)
+    for q in range(2 * NX):
+        turn_step(1, q)
     near_y = [y, yd, yu]
     product(1, near_y, 0, [0, 1])
     product(1, near_y, 0, [2, 3])
@@ -400,26 +406,32 @@
     product(1, near_y, 1, [xr])
     turn_end(1)
     product(0, every, 1, [xo])
+
+    def other_core(e):
+        return remote(gram.at[:, e, 1 - core], r1.at[e], a_s.at[e], a_r.at[e], partner)
+
+    def to_owner(n):
+        return remote(rz.at[n % 2, n // 2], r3.at[z], c_s.at[0], c_r.at[0], (sink(n), y))
+
+    def to_owners(e):
+        other_core(e).wait_recv()
+        for yt in range(NY):
+            n = 2 * yt + e
+            rz[e, yt] = (r1[e, yt] + gram[yt, e, core]).astype(jnp.bfloat16)
+
+            @pl.when(sink(n) != me)
+            def _():
+                to_owner(n).start()
+
+    other_core(0).start()
     product(1, near_y, 1, [xo])
     product(1, [yo], 0, [0, 1])
     product(1, [yo], 0, [2, 3])
+    to_owners(0)
     product(1, [yo], 1, [x, xl])
     product(1, [yo], 1, [xr, xo])
-
-    other = remote(gram.at[:, :, 1 - core], r1, a_s.at[0], a_r.at[0], partner)
-    other.start()
-
-    def to_owner(n):
-        return remote(rz.at[n // 2, n % 2], r3.at[z], c_s.at[0], c_r.at[0], (sink(n), y))
-
-    other.wait_recv()
-    for n in range(nz):
-        both = r1[n // 2, n % 2] + gram[n // 2, n % 2, core]
-        rz[n // 2, n % 2] = both.astype(jnp.bfloat16)
-
-        @pl.when(sink(n) != me)
-        def _():
-            to_owner(n).start()
+    other_core(1).start()
+    to_owners(1)
 
     for xt in range(NX):
         cols = pl.ds(xt * BL, BL)
@@ -431,14 +443,15 @@
     own_out = pltpu.make_async_copy(whole, out, loc.at[0])
     own_out.start()
     for h in range(2):
-        several(sx.at[h, pl.ds(0, 3)], g_s.at[h, 0], g_r.at[h, 0, 0, 4]).wait_send()
-        several(st.at[h, pl.ds(0, 3)], g_s.at[h, 1], g_r.at[h, 1, 0, 4]).wait_send()
+        several(sx.at[h, pl.ds(0, 3)], g_s.at[h, 0], g_r.at[h, 0, 0, 8]).wait_send()
+        several(st.at[h, pl.ds(0, 3)], g_s.at[h, 1], g_r.at[h, 1, 0, 8]).wait_send()
     sends_done(2, x1b)
-    other.wait_send()
+    for e in range(2):
+        other_core(e).wait_send()
 
     @pl.when(source(z) == me)
     def _():
-        r3[z] = rz[z // 2, lax.rem(x, 2)]
+        r3[z] = rz[lax.rem(x, 2), z // 2]
 
     def all_sums(do):
         @pl.when(source(z) == me)
@@ -486,17 +499,17 @@
             pltpu.VMEM((2, NY, BL, NX * HALF * BL), jnp.bfloat16),
             pltpu.VMEM((BLK, BL, NX * BL), jnp.bfloat16),
             pltpu.VMEM((NY, 2, 2, 32, NX * BL), jnp.float32),
-            pltpu.VMEM((NY, 2, 32, NX * BL), jnp.float32),
-            pltpu.VMEM((NY, 2, 32, NX * BL), jnp.bfloat16),
+            pltpu.VMEM((2, NY, 32, NX * BL), jnp.float32),
+            pltpu.VMEM((2, NY, 32, NX * BL), jnp.bfloat16),
             pltpu.VMEM((nz, 32, NX * BL), jnp.bfloat16),
             dma((5,)),
             dma((1,)), dma((3,)),
             dma((1,)), dma((1,)),
             dma((1,)), dma((2, 4)), dma((2, 2)), dma((1,)),
-            dma((3,)), dma((2, 2, flow_len)),
+            dma((3,)), dma((2, 2, 2 * flow_len)),
             dma((3,)), dma((3,)),
-            dma((2, 2)), dma((2, 2, 2, 5)),
-            dma((1,)), dma((1,)),
+            dma((2, 2)), dma((2, 2, 2, 9)),
+            dma((2,)), dma((2,)),
             dma((1,)), dma((1,)),
         ],
         compiler_params=pltpu.CompilerParams(
@@ -505,11 +518,29 @@
     )(expression, affinity, near, far, count)
 
 
+def last_kernel(smoothed, covariance, smoothed_out, covariance_out):
+    smoothed_out[...] = smoothed[...]
+    covariance_out[...] = covariance[...]
+
+
+def hand_over(smoothed, covariance):
+    vmem = pl.BlockSpec(memory_space=pltpu.VMEM)
+    return pl.pallas_call(
+        last_kernel,
+        out_shape=(
+            jax.ShapeDtypeStruct(smoothed.shape, smoothed.dtype),
+            jax.ShapeDtypeStruct(covariance.shape, covariance.dtype),
+        ),
+        in_specs=[vmem, vmem],
+        out_specs=(vmem, vmem),
+    )(smoothed, covariance)
+
+
 def body(nz, expression, affinity, near_blocks, far_blocks, far_count):
     blocks = expression.reshape(BLK, BL, expression.shape[1])
-    current, covariance = diffuse(
+    current, covariance = hand_over(*diffuse(
         blocks, affinity, near_blocks.T, far_blocks, far_count, nz
-    )
+    ))
     return (current.reshape(expression.shape), covariance)
 
 

time: 219 us -> 216 us (0.986); the launches traced: 219 us -> 212 us
  Pallas kernels: 215 us -> 211 us
  local copies, waits for them, and re-layouts: 3.74 us -> 0 us
    pallas_call x1, Pallas kernels: 215 us -> 209 us  [diffuse(): pl.pallas_call(functools.partial(diffuse_kernel, nz, 1.0 / (shards * BLK...]
    unnamed x2 -> x0, local copies, waits for them, and re-layouts: 3.74 us -> none
    pallas_call x0 -> x1, Pallas kernels: none -> 2.27 us  [hand_over(): pl.pallas_call(last_kernel, out_shape=(jax.ShapeDtypeStruct(smoothed.shap...]
where the time goes in v8:
time: 216 us; the launch traced here: 212 us
  Pallas kernels  211 us (98%)
    pallas_call x1, Pallas kernels, diffuse(): pl.pallas_call(functools.partial(diffuse_kernel, nz, 1.0 / (shards * BLK...  209 us

profile of v8, /device:TPU:33, one launch (start us, length us, event | category | flops | bytes accessed | tf_op | source)
XLA Modules:
  0.0 211.7 jit_solution(11312625713007992564)
XLA Ops:
  0.6 208.8 %shard_map.68 = (bf16[8,128,512]{2,1,0:T(8,128)(2,1)}, f32[32,512]{1,0:T(8,128)}) custom-call(bf16[8,128,512]{2,1,0:T(8,128)(2,1)} %bitcast.3, bf16[8,12,128,128]{3,2,1,0:T(8,128)(2,1)} %aff.1, s32[4,8]{1,0:T(4,128)} %bitcast.4, s32[8,8]{1,0:T(8,128)} %far.1, s32[8]{0:T(128)} %count.1), custom_call_target="tpu_custom_call" | custom-call | tf_op jit(solution)/shard_map/pallas_call | solution.py:479
  209.4 2.3 %shard_map.69 = (bf16[8,128,512]{2,1,0:T(8,128)(2,1)}, f32[32,512]{1,0:T(8,128)}) custom-call(bf16[8,128,512]{2,1,0:T(8,128)(2,1)} %get-tuple-element.6.smoothed, f32[32,512]{1,0:T(8,128)} %get-tuple-element.7.covariance), custom_call_target="tpu_custom_call" | custom-call | tf_op jit(solution)/shard_map/pallas_call | solution.py:528

commit v9 on v8

--- a/solution.py
+++ b/solution.py
@@ -51,8 +51,8 @@
     up = (me, wrap(y + 1, NY))
     down = (me, wrap(y - 1, NY))
 
-    def sink(n):
-        return cell(2 * (n // 2) + x // 2, 2 * lax.rem(x, 2) + n % 2, core)
+    def sink(yt, e):
+        return cell(2 * yt + x // 2, 2 * lax.rem(x, 2) + e, core)
 
     def source(zz):
         return cell(zz, 2 * lax.rem(z, 2) + x // 2, core)
@@ -72,9 +72,11 @@
     def columns(ref, xx):
         return ref.at[:, :, pl.ds(pl.multiple_of(xx * BL, BL), BL)]
 
-    def deal(d):
+    def deal(d, u):
+        rows = pl.ds(HALF * u, HALF)
         return remote(
-            columns(expr, wrap(x + d, NX)), piece(x0, me), xs_s.at[0], xs_r.at[d - 1], x_dev(d)
+            columns(expr, wrap(x + d, NX)).at[rows], piece(x0, me).at[rows],
+            xs_s.at[0], xs_r.at[d - 1, u], x_dev(d),
         )
 
     own_in = pltpu.make_async_copy(columns(expr, x), piece(x0, me), loc.at[0])
@@ -114,22 +116,18 @@
                 w_forward(way, n - 4).wait_recv()
                 w_across(2, i).start()
 
-    def unit(n):
-        return NX if n == 0 else 2 * NX
-
-    def flow_len(n):
-        return unit(n) * (nz // 2) - unit(n) // 2
+    unit = 2 * NX
+    flow_len = unit * (nz // 2) - unit // 2
 
     def shard_of(zz, j, kk):
         return cell(wrap(zz, nz), wrap(x - j, NX), kk)
 
     def place(n, zz, q, kk):
-        if n == 0:
-            return shard_of(zz, q, kk) * BLK
-        return shard_of(zz, q // 2, kk) * HALF + 2 * lax.rem(q, 2)
+        shard, upper = shard_of(zz, q // 2, kk), lax.rem(q, 2)
+        return shard * BLK + HALF * upper if n == 0 else shard * HALF + 2 * upper
 
     def part_of(n, buf, first):
-        return buf.at[pl.ds(first, BLK if n == 0 else 2)]
+        return buf.at[pl.ds(first, HALF if n == 0 else 2)]
 
     def z_copy(n, buf, way, s, first):
         ref = part_of(n, buf, first)
@@ -142,12 +140,12 @@
         return remote(ref, ref, p_s.at[n], p_r.at[n], partner)
 
     def from_left(n, r, kk):
-        return place(n, z - 1 - r // unit(n), lax.rem(r, unit(n)), kk)
+        return place(n, z - 1 - r // unit, lax.rem(r, unit), kk)
 
     def from_right(n, r, kk):
-        half_unit = unit(n) // 2
-        q = lax.rem(r, unit(n)) + jnp.where(r < flow_len(n) - half_unit, 0, half_unit)
-        return place(n, z + 1 + r // unit(n), q, kk)
+        half_unit = unit // 2
+        q = lax.rem(r, unit) + jnp.where(r < flow_len - half_unit, 0, half_unit)
+        return place(n, z + 1 + r // unit, q, kk)
 
     def send_own(n, buf, q):
         first = place(n, z, q, core)
@@ -156,7 +154,7 @@
         p_copy(n, buf, first).start()
 
     def pass_step(n, buf, r):
-        size, last = unit(n), flow_len(n)
+        size, last = unit, flow_len
         first = from_left(n, r, core)
         z_copy(n, buf, 0, r, first).wait_recv()
 
@@ -187,12 +185,12 @@
         return remote(ref, ref, send, recv, partner)
 
     def partner_done(n, buf):
-        size = (BLK if n == 0 else 2) * (unit(n) + 2 * flow_len(n))
+        size = (HALF if n == 0 else 2) * (unit + 2 * flow_len)
         several(buf.at[pl.ds(0, size)], p_s.at[n], p_r.at[n]).wait_recv()
 
     def sends_done(n, buf):
-        size = BLK if n == 0 else 2
-        z_all, p_all = size * 2 * flow_len(n), size * (unit(n) + 2 * flow_len(n))
+        size = HALF if n == 0 else 2
+        z_all, p_all = size * 2 * flow_len, size * (unit + 2 * flow_len)
         several(buf.at[pl.ds(0, z_all)], z_s.at[n], p_r.at[n]).wait_send()
         several(buf.at[pl.ds(0, p_all)], p_s.at[n], p_r.at[n]).wait_send()
 
@@ -262,17 +260,19 @@
     pl.semaphore_wait(barrier, len(peers) + nz - jnp.where(source(z) == me, 1, 0))
 
     send_own(0, x0, 0)
-    for d in (1, 3, 2):
-        deal(d).start()
+    send_own(0, x0, 1)
+    for u in range(2):
+        for d in (1, 3, 2):
+            deal(d, u).start()
     for d in (1, 2, 3):
         names(d).start()
     for n in range(4):
         w_first(0, n).start()
         w_first(1, n).start()
-    for j in (1, 3, 2):
-        deal(j).wait_recv()
-        send_own(0, x0, j)
-    cuts = (0, 4, 6, 8, 9, 11, 12)
+    for j, u in ((1, 0), (3, 0), (1, 1), (3, 1), (2, 0), (2, 1)):
+        deal(j, u).wait_recv()
+        send_own(0, x0, 2 * j + u)
+    cuts = (0, 8, 12, 16, 18, 22, 24)
     for part in range(6):
         pass_on(0, x0, cuts[part], cuts[part + 1])
         w_serve(part)
@@ -281,7 +281,7 @@
     to_smem.start()
     to_smem.wait()
     own_w.wait()
-    pass_on(0, x0, 12, flow_len(0))
+    pass_on(0, x0, 24, flow_len)
     several(w.at[pl.ds(0, 3), pl.ds(0, 4)], w_s.at[0], wy_r.at[0]).wait_recv()
     partner_done(0, x0)
 
@@ -299,7 +299,7 @@
     sends_done(0, x0)
     pass_on(1, x1a, 16, 20)
 
-    @pl.loop(20, flow_len(1))
+    @pl.loop(20, flow_len)
     def _(r):
         pass_step(1, x1a, r)
         send_own(2, x1b, r - 20)
@@ -310,14 +310,14 @@
         return min(n, 8) if isinstance(n, int) else n
 
     def turn_x(h, way, n, xt, q):
-        ref = sx.at[h, xt, wrap(xt - q // 2, NX), pl.ds(2 * (q % 2), 2)]
+        ref = sx.at[h, xt, q // 2, pl.ds(2 * (q % 2), 2)]
         return remote(
             ref, ref, g_s.at[h, 0], g_r.at[h, 0, way, passed(n)], x_dev(1 if way == 0 else 3)
         )
 
     def turn_y(h, way, n, yt, q):
-        first = wrap(x - q // 2, NX) * 2 + q % 2
-        ref = st.at[h, yt, :, pl.ds(pl.multiple_of(first * 2 * BL, 2 * BL), 2 * BL)]
+        cells = pl.ds(q * 2 * BL if isinstance(q, int) else pl.multiple_of(q * 2 * BL, 2 * BL), 2 * BL)
+        ref = st.at[h, yt, :, cells]
         return remote(
             ref, ref, g_s.at[h, 1], g_r.at[h, 1, way, passed(n)], up if way == 0 else down
         )
@@ -342,34 +342,38 @@
             turn_x(h, 1, 4 + q, xr, q).start()
             turn_y(h, 1, 4 + q, yu, q).start()
 
-    def turn_end(h):
-        for way in range(2):
-            several(sx.at[h, 0, pl.ds(0, 2)], g_s.at[h, 0], g_r.at[h, 0, way, 8]).wait_recv()
-            several(st.at[h, 0, :, pl.ds(0, 2 * HALF * BL)], g_s.at[h, 1], g_r.at[h, 1, way, 8]).wait_recv()
-
-    def product(hr, yts, hc, xts):
-        lhs = jnp.concatenate([st[hr, yt] for yt in yts], axis=0)
+    def turn_end(h, way):
+        several(sx.at[h, 0, pl.ds(0, 2)], g_s.at[h, 0], g_r.at[h, 0, way, 8]).wait_recv()
+        several(st.at[h, 0, :, pl.ds(0, 2 * HALF * BL)], g_s.at[h, 1], g_r.at[h, 1, way, 8]).wait_recv()
+
+    ys, xs_all = (y, yd, yu, yo), (x, xl, xr, xo)
+
+    def product(part, hr, rows, hc, cols):
+        cells = 2 * HALF * BL
+        lhs = jnp.concatenate([st[hr, ys[r], :, pl.ds(part * cells, cells)] for r in rows], axis=0)
         rhs = jnp.concatenate(
-            [sx[hc, xt].reshape(NX * HALF * BL, BL) for xt in xts], axis=1
-        )
-        part = jnp.dot(lhs, rhs, preferred_element_type=jnp.float32)
+            [sx[hc, xs_all[c], pl.ds(2 * part, 2)].reshape(cells, BL) for c in cols], axis=1
+        )
+        sums = jnp.dot(lhs, rhs, preferred_element_type=jnp.float32)
         mid = BL // 2
-        for i, yt in enumerate(yts):
-            for k, xt in enumerate(xts):
-                cols = pl.ds(xt * BL if isinstance(xt, int) else pl.multiple_of(xt * BL, BL), BL)
-                upper = part[i * BL:i * BL + mid, k * BL:(k + 1) * BL]
-                lower = part[i * BL + mid:(i + 1) * BL, k * BL:(k + 1) * BL]
-                if hc == 0:
-                    tile = (upper + swap(lower)).reshape(2, 32, BL)
+        mine = on_left[0:mid] if hc == 0 else jnp.logical_not(on_left[0:mid])
+        for i, r in enumerate(rows):
+            for k, c in enumerate(cols):
+                at = pl.ds(c * BL, BL)
+                upper = sums[i * BL:i * BL + mid, k * BL:(k + 1) * BL]
+                lower = sums[i * BL + mid:(i + 1) * BL, k * BL:(k + 1) * BL]
+                tile = upper + swap(lower) if hc == 0 else swap(upper) + lower
+                if part == 0 and hc == 0:
+                    gram[r, hr, :, :, at] = tile.reshape(2, 32, BL)
                 else:
-                    tile = (swap(upper) + lower).reshape(2, 32, BL)
-                    tile = jnp.where(on_left[0:mid].reshape(2, 32, BL), gram[yt, hr, :, :, cols], tile)
-                gram[yt, hr, :, :, cols] = tile
+                    old = gram[r, hr, :, :, at].reshape(mid, BL)
+                    new = tile if part == 0 else old + tile
+                    gram[r, hr, :, :, at] = jnp.where(mine, new, old).reshape(2, 32, BL)
 
     @pl.loop(0, 16)
     def _(r):
         pass_step(2, x1b, r)
-        step_two(0, wrap(x - r // 4, NX), lax.rem(r, 4))
+        step_two(0, r // 4, lax.rem(r, 4))
 
         @pl.when(lax.rem(r, 2) == 1)
         def _():
@@ -382,55 +386,80 @@
     pass_on(2, x1b, 22, 26)
     for q in range(4, 8):
         turn_step(0, q)
-    pass_on(2, x1b, 26, flow_len(2))
+    pass_on(2, x1b, 26, flow_len)
     partner_done(2, x1b)
 
     @pl.loop(0, 2 * NX)
     def _(q):
         for i in range(2):
-            step_two(1, wrap(x - q // 2, NX), 2 * lax.rem(q, 2) + i)
+            step_two(1, q // 2, 2 * lax.rem(q, 2) + i)
         turn_own(1, q)
 
-    turn_end(0)
-    every = list(range(NY))
-    product(0, every, 0, [0, 1])
-    product(0, every, 0, [2, 3])
+    turn_end(0, 0)
+    turn_end(0, 1)
+    every, near_y = [0, 1, 2, 3], [0, 1, 2]
+    for part in range(2):
+        product(part, 0, every, 0, [0, 1])
+        product(part, 0, every, 0, [2, 3])
+
+    def early(part):
+        product(part, 1, near_y, 0, [0, 1])
+        product(part, 1, near_y, 0, [2, 3])
+        product(part, 0, every, 1, [0, 1])
+        product(part, 0, every, 1, [2])
+        product(part, 1, near_y, 1, [0, 1])
+        product(part, 1, near_y, 1, [2])
+
+    def late(part):
+        product(part, 0, every, 1, [3])
+        product(part, 1, near_y, 1, [3])
+        product(part, 1, [3], 0, [0, 1])
+        product(part, 1, [3], 0, [2, 3])
+        product(part, 1, [3], 1, [0, 1])
+        product(part, 1, [3], 1, [2, 3])
+
+    old_cols, new_cols, all_cols = pl.ds(0, 3 * BL), pl.ds(3 * BL, BL), pl.ds(0, NX * BL)
+    rounds = (
+        ((0, 0, 4, old_cols), (1, 0, 3, old_cols)),
+        ((0, 0, 4, new_cols), (1, 0, 3, new_cols), (1, 3, 1, all_cols)),
+    )
+
+    def other_core(i, k):
+        e, first, size, at = rounds[i][k]
+        rows = pl.ds(first, size)
+        return remote(
+            gram.at[rows, e, 1 - core, :, at], r1.at[e, rows, :, at],
+            a_s.at[2 * i + k], a_r.at[2 * i + k], partner,
+        )
+
+    def to_cores(i):
+        for k in range(len(rounds[i])):
+            other_core(i, k).start()
+
+    def to_owners(i):
+        for k, (e, first, size, at) in enumerate(rounds[i]):
+            other_core(i, k).wait_recv()
+            for r in range(first, first + size):
+                rz[e, r, :, at] = (r1[e, r, :, at] + gram[r, e, core, :, at]).astype(jnp.bfloat16)
+                owner = sink(ys[r], e)
+
+                @pl.when(owner != me)
+                def _():
+                    remote(
+                        rz.at[e, r, :, at], r3.at[z, :, at], c_s.at[0], c_r.at[0], (owner, y)
+                    ).start()
+
     for q in range(2 * NX):
         turn_step(1, q)
-    near_y = [y, yd, yu]
-    product(1, near_y, 0, [0, 1])
-    product(1, near_y, 0, [2, 3])
-    product(0, every, 1, [x, xl])
-    product(0, every, 1, [xr])
-    product(1, near_y, 1, [x, xl])
-    product(1, near_y, 1, [xr])
-    turn_end(1)
-    product(0, every, 1, [xo])
-
-    def other_core(e):
-        return remote(gram.at[:, e, 1 - core], r1.at[e], a_s.at[e], a_r.at[e], partner)
-
-    def to_owner(n):
-        return remote(rz.at[n % 2, n // 2], r3.at[z], c_s.at[0], c_r.at[0], (sink(n), y))
-
-    def to_owners(e):
-        other_core(e).wait_recv()
-        for yt in range(NY):
-            n = 2 * yt + e
-            rz[e, yt] = (r1[e, yt] + gram[yt, e, core]).astype(jnp.bfloat16)
-
-            @pl.when(sink(n) != me)
-            def _():
-                to_owner(n).start()
-
-    other_core(0).start()
-    product(1, near_y, 1, [xo])
-    product(1, [yo], 0, [0, 1])
-    product(1, [yo], 0, [2, 3])
+    early(0)
+    early(1)
+    to_cores(0)
+    turn_end(1, 0)
+    late(0)
     to_owners(0)
-    product(1, [yo], 1, [x, xl])
-    product(1, [yo], 1, [xr, xo])
-    other_core(1).start()
+    turn_end(1, 1)
+    late(1)
+    to_cores(1)
     to_owners(1)
 
     for xt in range(NX):
@@ -446,12 +475,14 @@
         several(sx.at[h, pl.ds(0, 3)], g_s.at[h, 0], g_r.at[h, 0, 0, 8]).wait_send()
         several(st.at[h, pl.ds(0, 3)], g_s.at[h, 1], g_r.at[h, 1, 0, 8]).wait_send()
     sends_done(2, x1b)
-    for e in range(2):
-        other_core(e).wait_send()
+    for i in range(2):
+        for k in range(len(rounds[i])):
+            other_core(i, k).wait_send()
 
     @pl.when(source(z) == me)
     def _():
-        r3[z] = rz[lax.rem(x, 2), z // 2]
+        mine = z // 2
+        r3[z] = rz[lax.rem(x, 2), jnp.where(mine == y, 0, jnp.where(mine == yd, 1, jnp.where(mine == yu, 2, 3)))]
 
     def all_sums(do):
         @pl.when(source(z) == me)
@@ -466,14 +497,17 @@
     total = r3[0].astype(jnp.float32)
     for zz in range(1, nz):
         total += r3[zz].astype(jnp.float32)
-    cov[...] = total * scale
+    total = total * scale
+    from_x = 2 * lax.rem(z, 2) + x // 2
+    for c, shift in enumerate((0, NX - 1, 1, 2)):
+        cov[:, pl.ds(pl.multiple_of(lax.rem(from_x + shift, NX) * BL, BL), BL)] = total[:, c * BL:(c + 1) * BL]
     all_sums(lambda copies: copies.wait_send())
     own_out.wait()
 
 
 def diffuse(expression, affinity, near, far, count, nz):
     shards = nz * 2 * NX
-    flow_len = 4 * (nz // 2) - 2
+    flow_len = 2 * NX * (nz // 2) - NX
     dma = pltpu.SemaphoreType.DMA
     any_spec = pl.BlockSpec(memory_space=pl.ANY)
     return pl.pallas_call(
@@ -503,13 +537,13 @@
             pltpu.VMEM((2, NY, 32, NX * BL), jnp.bfloat16),
             pltpu.VMEM((nz, 32, NX * BL), jnp.bfloat16),
             dma((5,)),
-            dma((1,)), dma((3,)),
+            dma((1,)), dma((3, 2)),
             dma((1,)), dma((1,)),
             dma((1,)), dma((2, 4)), dma((2, 2)), dma((1,)),
-            dma((3,)), dma((2, 2, 2 * flow_len)),
+            dma((3,)), dma((2, 2, flow_len)),
             dma((3,)), dma((3,)),
             dma((2, 2)), dma((2, 2, 2, 9)),
-            dma((2,)), dma((2,)),
+            dma((5,)), dma((5,)),
             dma((1,)), dma((1,)),
         ],
         compiler_params=pltpu.CompilerParams(

time: 216 us -> 213 us (0.986); the launches traced: 212 us -> 212 us
  no operation moved by 1% of the time
where the time goes in v9:
time: 213 us; the launch traced here: 212 us
  Pallas kernels  212 us (100%)
    pallas_call x1, Pallas kernels, diffuse(): pl.pallas_call(functools.partial(diffuse_kernel, nz, 1.0 / (shards * BLK...  210 us

profile of v9, /device:TPU:33, one launch (start us, length us, event | category | flops | bytes accessed | tf_op | source)
XLA Modules:
  0.0 212.4 jit_solution(12623510013778820344)
XLA Ops:
  0.6 209.5 %shard_map.68 = (bf16[8,128,512]{2,1,0:T(8,128)(2,1)}, f32[32,512]{1,0:T(8,128)}) custom-call(bf16[8,128,512]{2,1,0:T(8,128)(2,1)} %bitcast.3, bf16[8,12,128,128]{3,2,1,0:T(8,128)(2,1)} %aff.1, s32[4,8]{1,0:T(4,128)} %bitcast.4, s32[8,8]{1,0:T(8,128)} %far.1, s32[8]{0:T(128)} %count.1), custom_call_target="tpu_custom_call" | custom-call | tf_op jit(solution)/shard_map/pallas_call | solution.py:513
  210.1 2.3 %shard_map.69 = (bf16[8,128,512]{2,1,0:T(8,128)(2,1)}, f32[32,512]{1,0:T(8,128)}) custom-call(bf16[8,128,512]{2,1,0:T(8,128)(2,1)} %get-tuple-element.6.smoothed, f32[32,512]{1,0:T(8,128)} %get-tuple-element.7.covariance), custom_call_target="tpu_custom_call" | custom-call | tf_op jit(solution)/shard_map/pallas_call | solution.py:562

commit v10 on v9

--- a/solution.py
+++ b/solution.py
@@ -13,6 +13,7 @@
 BL = 128
 BLK = 8
 SLOTS = 12
+CHUNKS = 4
 LOC = 4
 HALF = BLK // 2
 
@@ -272,7 +273,7 @@
     for j, u in ((1, 0), (3, 0), (1, 1), (3, 1), (2, 0), (2, 1)):
         deal(j, u).wait_recv()
         send_own(0, x0, 2 * j + u)
-    cuts = (0, 8, 12, 16, 18, 22, 24)
+    cuts = (0, 7, 11, 15, 17, 21, 24)
     for part in range(6):
         pass_on(0, x0, cuts[part], cuts[part + 1])
         w_serve(part)
@@ -297,13 +298,14 @@
     several(lv.at[pl.ds(0, NX - 1)], li_s.at[0], li_r.at[0]).wait_send()
     several(w.at[pl.ds(0, 3)], w_s.at[0], wy_r.at[0]).wait_send()
     sends_done(0, x0)
-    pass_on(1, x1a, 16, 20)
-
-    @pl.loop(20, flow_len)
+    pass_on(1, x1a, 16, 19)
+
+    @pl.loop(19, flow_len - 1)
     def _(r):
         pass_step(1, x1a, r)
-        send_own(2, x1b, r - 20)
-
+        send_own(2, x1b, r - 19)
+
+    pass_on(1, x1a, flow_len - 1, flow_len)
     partner_done(1, x1a)
 
     def passed(n):
@@ -348,27 +350,22 @@
 
     ys, xs_all = (y, yd, yu, yo), (x, xl, xr, xo)
 
-    def product(part, hr, rows, hc, cols):
-        cells = 2 * HALF * BL
-        lhs = jnp.concatenate([st[hr, ys[r], :, pl.ds(part * cells, cells)] for r in rows], axis=0)
+    def product(hr, rows, hc, cols):
+        lhs = jnp.concatenate([st[hr, ys[r]] for r in rows], axis=0)
         rhs = jnp.concatenate(
-            [sx[hc, xs_all[c], pl.ds(2 * part, 2)].reshape(cells, BL) for c in cols], axis=1
+            [sx[hc, xs_all[c]].reshape(NX * HALF * BL, BL) for c in cols], axis=1
         )
         sums = jnp.dot(lhs, rhs, preferred_element_type=jnp.float32)
         mid = BL // 2
-        mine = on_left[0:mid] if hc == 0 else jnp.logical_not(on_left[0:mid])
         for i, r in enumerate(rows):
             for k, c in enumerate(cols):
                 at = pl.ds(c * BL, BL)
                 upper = sums[i * BL:i * BL + mid, k * BL:(k + 1) * BL]
                 lower = sums[i * BL + mid:(i + 1) * BL, k * BL:(k + 1) * BL]
                 tile = upper + swap(lower) if hc == 0 else swap(upper) + lower
-                if part == 0 and hc == 0:
-                    gram[r, hr, :, :, at] = tile.reshape(2, 32, BL)
-                else:
-                    old = gram[r, hr, :, :, at].reshape(mid, BL)
-                    new = tile if part == 0 else old + tile
-                    gram[r, hr, :, :, at] = jnp.where(mine, new, old).reshape(2, 32, BL)
+                if hc == 1:
+                    tile = jnp.where(on_left[0:mid], gram[r, hr, :, :, at].reshape(mid, BL), tile)
+                gram[r, hr, :, :, at] = tile.reshape(2, 32, BL)
 
     @pl.loop(0, 16)
     def _(r):
@@ -398,25 +395,24 @@
     turn_end(0, 0)
     turn_end(0, 1)
     every, near_y = [0, 1, 2, 3], [0, 1, 2]
-    for part in range(2):
-        product(part, 0, every, 0, [0, 1])
-        product(part, 0, every, 0, [2, 3])
-
-    def early(part):
-        product(part, 1, near_y, 0, [0, 1])
-        product(part, 1, near_y, 0, [2, 3])
-        product(part, 0, every, 1, [0, 1])
-        product(part, 0, every, 1, [2])
-        product(part, 1, near_y, 1, [0, 1])
-        product(part, 1, near_y, 1, [2])
-
-    def late(part):
-        product(part, 0, every, 1, [3])
-        product(part, 1, near_y, 1, [3])
-        product(part, 1, [3], 0, [0, 1])
-        product(part, 1, [3], 0, [2, 3])
-        product(part, 1, [3], 1, [0, 1])
-        product(part, 1, [3], 1, [2, 3])
+    product(0, every, 0, [0, 1])
+    product(0, every, 0, [2, 3])
+
+    def early():
+        product(1, near_y, 0, [0, 1])
+        product(1, near_y, 0, [2, 3])
+        product(0, every, 1, [0, 1])
+        product(0, every, 1, [2])
+        product(1, near_y, 1, [0, 1])
+        product(1, near_y, 1, [2])
+
+    def late():
+        product(0, every, 1, [3])
+        product(1, near_y, 1, [3])
+        product(1, [3], 0, [0, 1])
+        product(1, [3], 0, [2, 3])
+        product(1, [3], 1, [0, 1])
+        product(1, [3], 1, [2, 3])
 
     old_cols, new_cols, all_cols = pl.ds(0, 3 * BL), pl.ds(3 * BL, BL), pl.ds(0, NX * BL)
     rounds = (
@@ -451,14 +447,12 @@
 
     for q in range(2 * NX):
         turn_step(1, q)
-    early(0)
-    early(1)
+    early()
     to_cores(0)
     turn_end(1, 0)
-    late(0)
     to_owners(0)
     turn_end(1, 1)
-    late(1)
+    late()
     to_cores(1)
     to_owners(1)
 
@@ -552,21 +546,37 @@
     )(expression, affinity, near, far, count)
 
 
-def last_kernel(smoothed, covariance, smoothed_out, covariance_out):
-    smoothed_out[...] = smoothed[...]
-    covariance_out[...] = covariance[...]
+def last_kernel(smoothed, covariance, smoothed_out, covariance_out, held, held_too, sems):
+    parts = [(covariance, held_too, covariance_out)]
+    for i in range(CHUNKS):
+        rows = pl.ds(i * (BLK // CHUNKS), BLK // CHUNKS)
+        parts.append((smoothed.at[rows], held.at[rows], smoothed_out.at[rows]))
+    ins = [pltpu.make_async_copy(p[0], p[1], sems.at[0, i]) for i, p in enumerate(parts)]
+    outs = [pltpu.make_async_copy(p[1], p[2], sems.at[1, i]) for i, p in enumerate(parts)]
+    for copy in ins:
+        copy.start()
+    for first, second in zip(ins, outs):
+        first.wait()
+        second.start()
+    for copy in outs:
+        copy.wait()
 
 
 def hand_over(smoothed, covariance):
-    vmem = pl.BlockSpec(memory_space=pltpu.VMEM)
+    any_spec = pl.BlockSpec(memory_space=pl.ANY)
     return pl.pallas_call(
         last_kernel,
         out_shape=(
             jax.ShapeDtypeStruct(smoothed.shape, smoothed.dtype),
             jax.ShapeDtypeStruct(covariance.shape, covariance.dtype),
         ),
-        in_specs=[vmem, vmem],
-        out_specs=(vmem, vmem),
+        in_specs=[any_spec, any_spec],
+        out_specs=(any_spec, any_spec),
+        scratch_shapes=[
+            pltpu.VMEM(smoothed.shape, smoothed.dtype),
+            pltpu.VMEM(covariance.shape, covariance.dtype),
+            pltpu.SemaphoreType.DMA((2, CHUNKS + 1)),
+        ],
     )(smoothed, covariance)
 
 

time: 213 us -> 212 us (level)
  no operation moved by 1% of the time
where the time goes in v10:
time: 212 us
  Pallas kernels  211 us (100%)
    pallas_call x1, Pallas kernels, diffuse(): pl.pallas_call(functools.partial(diffuse_kernel, nz, 1.0 / (shards * BLK...  209 us

profile of v10, /device:TPU:33, one launch (start us, length us, event | category | flops | bytes accessed | tf_op | source)
XLA Modules:
  0.0 212.1 jit_solution(1288149245492196950)
XLA Ops:
  0.6 209.4 %shard_map.68 = (bf16[8,128,512]{2,1,0:T(8,128)(2,1)}, f32[32,512]{1,0:T(8,128)}) custom-call(bf16[8,128,512]{2,1,0:T(8,128)(2,1)} %bitcast.3, bf16[8,12,128,128]{3,2,1,0:T(8,128)(2,1)} %aff.1, s32[4,8]{1,0:T(4,128)} %bitcast.4, s32[8,8]{1,0:T(8,128)} %far.1, s32[8]{0:T(128)} %count.1), custom_call_target="tpu_custom_call" | custom-call | tf_op jit(solution)/shard_map/pallas_call | solution.py:507
  210.1 2.0 shard_map.69
